TPU v7x, 128 devices: a whole 4x4x4 slice. The times are simulated.
128 devices in a mesh: coil: 4 (over x), frame: 32 (over z, y, core).
Axes of the slice: x: 4, y: 4, z: 4, core: 2. Of those that a mesh axis runs over, the one named last changes fastest.
Arguments:
- image: float32 [128, 32, 2, 32, 128], P(('coil', 'frame')), may hold values from -16 to 16
- sens: bfloat16 [16, 128, 2, 32, 128], P('coil'), may hold values from -3 to 3
- data: bfloat16 [16, 128, 32, 2, 32, 128], P('coil', None, 'frame'), may hold values from -6 to 6
- mask: int32 [32, 32, 128], P('frame'), may hold values 0 or 1
- start: float32 [2, 32, 8], replicated, may hold values from -6 to 6
Outputs:
- new_image: float32 [128, 32, 2, 32, 128], P(('coil', 'frame'))
- spectrum: float32 [8], replicated
All inputs are finite; a program needn't handle non-finite values. No bound on the sum of `mask` on one device may be relied on, other than what follows from the above.
Results may differ from a plain program's by a relative error of at most 0.014.
Values may be sent and summed in bfloat16 or wider, within the bound.
No kernel may reach another device: no remote copies, remote signals or barrier semaphores. Data moves between devices by JAX's collectives and lax.ppermute only.
A program may use at most 192 MiB of HBM per device.

v0:
```python
import math

import jax
import jax.numpy as jnp
import ml_dtypes
import numpy as np
from jax import lax
from jax.experimental import pallas as pl
from jax.experimental.pallas import tpu as pltpu
from jax.sharding import PartitionSpec as P

NX = 128
NY = 128
NZ = 32
FRAMES = 32
HALF = 16
EPSILON = 1e-06
BF = jnp.bfloat16
F32 = jnp.float32


def dft_tables(length):
    counter = np.arange(length)
    product = counter[:, None] * counter[None, :] % length
    angles = product.astype(np.float32) * np.float32(2.0 * math.pi / length)
    factor = np.float32(1.0 / math.sqrt(length))
    return np.cos(angles) * factor, np.sin(angles) * factor


def wide_table(sign):
    c, s = dft_tables(NY)
    return np.block([[c, sign * s], [-sign * s, c]]).astype(ml_dtypes.bfloat16)


def deep_table(sign):
    c, s = dft_tables(NZ)
    one = np.block([[c, -sign * s], [sign * s, c]])
    return np.kron(np.eye(4, dtype=np.float32), one).astype(ml_dtypes.bfloat16)


def to_deep(a):
    out = []
    for j in range(0, a.shape[0], 256):
        one = a[j : j + 256].reshape(8, NZ, 2 * NY)
        one = jnp.concatenate([one[:, :, :NY], one[:, :, NY:]], axis=1).reshape(512, NY)
        out += [one[:256], one[256:]]
    return jnp.concatenate(out, axis=1)


def from_deep(k):
    k = jnp.concatenate([k[:, j : j + NY] for j in range(0, k.shape[1], NY)], axis=0)
    k = k.reshape(-1, 2 * NZ, NY)
    return k[:, :NZ], k[:, NZ:]


def grad_kernel(coil_ref, *refs):
    steps = (len(refs) - 4) // 2
    images, refs = refs[:steps], refs[steps:]
    sens_ref, data_ref, mask_ref, tables = refs[:4]
    outs = refs[4:]
    step = pl.program_id(0)
    coils = sens_ref.shape[0]
    span = HALF * NZ
    img = images[0][...]
    if steps == 2:
        img = jnp.where(step == 0, img, images[1][...])
    img = img.astype(F32)
    x_re, x_im = img[:, :NZ], img[:, NZ:]
    keep = mask_ref[0].astype(F32)[None]

    def sens(c):
        return sens_ref[c, :, 0].astype(F32), sens_ref[c, :, 1].astype(F32)

    def join(re, im):
        return jnp.concatenate([re, im], axis=-1).astype(BF).reshape(span, 2 * NY)

    u = []
    for c in range(coils):
        s_re, s_im = sens(c)
        u.append(join(s_re * x_re - s_im * x_im, s_re * x_im + s_im * x_re))
    a = jnp.dot(jnp.concatenate(u, axis=0), tables[0], preferred_element_type=F32).astype(BF)
    k = jnp.dot(tables[1], to_deep(a), preferred_element_type=F32)
    m = []
    for c in range(coils):
        k_re, k_im = from_deep(k[:, span * c : span * (c + 1)])
        k_re = keep * (k_re - data_ref[c, :, 0, 0].astype(F32))
        k_im = keep * (k_im - data_ref[c, :, 0, 1].astype(F32))
        m.append(join(k_re, k_im))
    b = jnp.dot(jnp.concatenate(m, axis=0), tables[2], preferred_element_type=F32).astype(BF)
    r = jnp.dot(tables[3], to_deep(b), preferred_element_type=F32)
    acc_re = acc_im = 0.0
    for c in range(coils):
        s_re, s_im = sens(c)
        r_re, r_im = from_deep(r[:, span * c : span * (c + 1)])
        acc_re += s_re * r_re + s_im * r_im
        acc_im += s_re * r_im - s_im * r_re
    total = jnp.concatenate([acc_re, acc_im], axis=1).astype(BF)
    for j in range(steps):

        @pl.when(step == j)
        def _(j=j):
            outs[j][...] = total


def coil_gradient(images, places, coil, sens, data, mask, room, weight=1):
    coils = sens.shape[0]
    rows = (HALF, 2 * NZ, NY)
    steps = len(images)
    (far, low), (far_next, low_next) = places[0], places[-1]

    def place(i, coil):
        return ((coil[0] + far + i * (far_next - far)) & 3) * 2 + low + i * (low_next - low)

    return pl.pallas_call(
        grad_kernel,
        grid_spec=pltpu.PrefetchScalarGridSpec(
            num_scalar_prefetch=1,
            grid=(steps,),
            in_specs=[pl.BlockSpec(rows, lambda i, o, block=block: (block, 0, 0)) for _, block in images]
            + [
                pl.BlockSpec((coils, HALF, 2, NZ, NY), lambda i, o: (0, place(i, o), 0, 0, 0)),
                pl.BlockSpec((coils, HALF, 1, 2, NZ, NY), lambda i, o: (0, place(i, o), 0, 0, 0, 0)),
                pl.BlockSpec((1, NZ, NY), lambda i, o: (0, 0, 0)),
            ]
            + [pl.BlockSpec((4, 256, 256), lambda i, o: (0, 0, 0))],
            out_specs=[pl.BlockSpec(rows, lambda i, o: (0, 0, 0))] * steps,
        ),
        out_shape=[jax.ShapeDtypeStruct(rows, BF)] * steps,
        cost_estimate=pl.CostEstimate(
            flops=weight * steps * HALF * coils * 32 * 2**20,
            bytes_accessed=steps * HALF * coils * 40000,
            transcendentals=0,
        ),
        compiler_params=pltpu.CompilerParams(vmem_limit_bytes=room * 2**20),
        name="coil_gradient",
    )(
        coil, *(x for x, _ in images), sens, data, mask,
        np.stack([wide_table(-1.0), deep_table(-1.0), wide_table(1.0), deep_table(1.0)]),
    )


SMALL = pltpu.CompilerParams(vmem_limit_bytes=8 * 2**20)


def total_of(refs):
    return sum(ref[...].astype(F32) for ref in refs).astype(BF)


def pair_kernel(a, b, out):
    out[...] = total_of((a, b))


def pair_sum(a, b):
    return pl.pallas_call(
        pair_kernel, out_shape=jax.ShapeDtypeStruct(a.shape, BF), compiler_params=SMALL, name="pair_sum",
    )(a, b)


def join_kernel(a0, b0, c0, a1, b1, c1, out_ref):
    out_ref[:HALF] = total_of((a0, b0, c0))
    out_ref[HALF:] = total_of((a1, b1, c1))


def join_sums(first, second):
    return pl.pallas_call(
        join_kernel, out_shape=jax.ShapeDtypeStruct((2 * HALF, 2 * NZ, NY), BF),
        compiler_params=SMALL, name="join_sums",
    )(*first, *second)


def gram_kernel(g_ref, gt_ref, q_ref, wide):
    wide[...] = g_ref[...].reshape(FRAMES * 2 * NZ, NY).astype(F32)
    total = jnp.zeros((2 * FRAMES, 2 * FRAMES), F32)
    for z in range(0, NZ, 2):
        pair = []
        for d in (z, z + 1):
            re = wide[pl.ds(d, FRAMES, stride=2 * NZ), :]
            im = wide[pl.ds(NZ + d, FRAMES, stride=2 * NZ), :]
            block = jnp.concatenate([re, im], axis=0).astype(BF)
            gt_ref[d] = block
            pair.append(block)
        both = jnp.concatenate(pair, axis=1)
        total += lax.dot_general(both, both, (((1,), (1,)), ((), ())), preferred_element_type=F32)
    h_re = total[:FRAMES, :FRAMES] + total[FRAMES:, FRAMES:]
    h_im = total[:FRAMES, FRAMES:] - total[FRAMES:, :FRAMES]
    row = lax.broadcasted_iota(jnp.int32, (FRAMES, FRAMES), 0)
    col = lax.broadcasted_iota(jnp.int32, (FRAMES, FRAMES), 1)
    q = jnp.where(row <= col, h_re, h_im)
    q_ref[...] = jnp.concatenate([q[8 * j : 8 * j + 8] for j in range(4)], axis=1)


def gram(g):
    return pl.pallas_call(
        gram_kernel,
        out_shape=(
            jax.ShapeDtypeStruct((NZ, 2 * FRAMES, NY), BF),
            jax.ShapeDtypeStruct((8, 128), F32),
        ),
        scratch_shapes=[pltpu.VMEM((FRAMES * 2 * NZ, NY), F32)],
        compiler_params=pltpu.CompilerParams(vmem_limit_bytes=32 * 2**20),
        name="gram",
    )(g)


def exact(a, b, dims=((1,), (0,))):
    return lax.dot_general(
        a, b, (dims, ((), ())), precision=lax.Precision.HIGHEST, preferred_element_type=F32
    )


def final_kernel(q0, q1, q2, q3, start_ref, gt_ref, image_ref, out_ref, spec_ref, wide):
    packed = (q0[...] + q1[...]) + (q2[...] + q3[...])
    q = jnp.concatenate([packed[:, 32 * j : 32 * j + 32] for j in range(4)], axis=0)
    qt = q.T
    row = lax.broadcasted_iota(jnp.int32, (FRAMES, FRAMES), 0)
    col = lax.broadcasted_iota(jnp.int32, (FRAMES, FRAMES), 1)
    h_re = jnp.where(row <= col, q, qt)
    h_im = jnp.where(row > col, q, jnp.where(row < col, -qt, 0.0))
    v_re, v_im = start_ref[0], start_ref[1]
    w_re = exact(h_re, v_re) - exact(h_im, v_im)
    w_im = exact(h_re, v_im) + exact(h_im, v_re)
    length = jnp.sqrt(jnp.sum(w_re * w_re + w_im * w_im, axis=0, keepdims=True) + EPSILON)
    v_re, v_im = w_re / length, w_im / length
    w_re = exact(h_re, v_re) - exact(h_im, v_im)
    w_im = exact(h_re, v_im) + exact(h_im, v_re)
    power = jnp.maximum(jnp.sum(v_re * w_re + v_im * w_im, axis=0, keepdims=True), 0.0)
    last = jnp.sum(w_re * w_re + w_im * w_im, axis=0, keepdims=True)
    spec_ref[...] = jnp.sqrt(last + EPSILON) / jnp.sqrt(power + EPSILON)
    total = jnp.sum(power, axis=1, keepdims=True)
    scale = 0.5 * math.sqrt(NX * NY * NZ * FRAMES) / jnp.sqrt(total)
    lanes = ((1,), (1,))
    t_re = (exact(v_re, v_re, lanes) + exact(v_im, v_im, lanes)) * scale
    t_im = (exact(v_im, v_re, lanes) - exact(v_re, v_im, lanes)) * scale
    left = jnp.concatenate(
        [jnp.concatenate([t_re, t_im], axis=1), jnp.concatenate([-t_im, t_re], axis=1)], axis=0
    )
    high = left.astype(BF)
    low = (left - high.astype(F32)).astype(BF)
    left = jnp.concatenate([high, low], axis=1)
    for z in range(NZ):
        block = gt_ref[z]
        update = jnp.dot(left, jnp.concatenate([block, block], axis=0), preferred_element_type=F32)
        wide[pl.ds(z, FRAMES, stride=2 * NZ), :] = update[:FRAMES]
        wide[pl.ds(NZ + z, FRAMES, stride=2 * NZ), :] = update[FRAMES:]
    out_ref[...] = 0.5 * image_ref[...] - wide[...].reshape(FRAMES, 2 * NZ, NY)


def finish(parts, start, gt, image):
    return pl.pallas_call(
        final_kernel,
        out_shape=(
            jax.ShapeDtypeStruct((FRAMES, 2 * NZ, NY), F32),
            jax.ShapeDtypeStruct((1, start.shape[2]), F32),
        ),
        scratch_shapes=[pltpu.VMEM((FRAMES * 2 * NZ, NY), F32)],
        compiler_params=pltpu.CompilerParams(vmem_limit_bytes=32 * 2**20),
        name="finish",
    )(*parts, start, gt, image)


RIGHT = [(i, (i + 1) % 4) for i in range(4)]
LEFT = [(i, (i + 3) % 4) for i in range(4)]


def after(x, *others):
    return lax.optimization_barrier((x,) + others)[0]


def local(image, sens, data, mask, start):
    flat = image.reshape(FRAMES, 2 * NZ, NY)
    coil = lax.axis_index("coil").astype(jnp.int32).reshape(1)

    def partial(images, places, *others, room=28):
        return coil_gradient(images, places, after(coil, *others), sens, data, mask, room)

    def right(x):
        return lax.ppermute(x, "coil", RIGHT)

    def left(x):
        return lax.ppermute(x, "coil", LEFT)

    own = lax.all_to_all(flat.astype(BF), "frame", split_axis=0, concat_axis=0, tiled=True)
    own0, own1 = own[:HALF], own[HALF:]
    left0, right1 = right(own0), left(own1)
    rows = [lax.dynamic_slice_in_dim(x, coil[0] * 2 * HALF, 2 * HALF, axis=1) for x in (sens, data)]
    g_own0, g_own1 = coil_gradient(
        [(own, 0), (own, 1)], [(0, 0), (0, 1)], jnp.zeros_like(coil), *rows, mask, 28, 2
    )
    left0, right1 = after(left0, g_own1, right1), after(right1, g_own1, left0)
    far0, far1 = right(left0), left(right1)
    g_left0, g_right1 = partial([(left0, 0), (right1, 0)], [(3, 0), (1, 1)])
    left1, right0 = right(after(own1, g_left0)), left(after(own0, g_left0))
    (g_far0,) = partial([(far0, 0)], [(2, 0)], g_left0)
    (g_far1,) = partial([(far1, 0)], [(2, 1)], g_far0)
    low, high = right(g_far0), left(g_far1)
    in_left1, in_right0 = right(after(g_right1, g_far1)), left(after(g_left0, g_far1))
    g_left1, g_right0 = partial([(left1, 0), (right0, 0)], [(3, 1), (1, 0)], g_far1)
    in_left0, in_right1 = right(pair_sum(g_right0, low)), left(pair_sum(g_left1, high))
    gradient = join_sums((g_own0, in_left0, in_right0), (g_own1, in_left1, in_right1))
    frames = lax.all_to_all(gradient, "frame", split_axis=0, concat_axis=0, tiled=True)
    gt, q = gram(frames)
    spread = lax.all_to_all(
        jnp.broadcast_to(q[None], (FRAMES, 8, 128)), "frame", split_axis=0, concat_axis=0, tiled=True
    )
    q = jnp.sum(spread, axis=0)
    parts = [q] + [lax.ppermute(q, "coil", [(i, i ^ d) for i in range(4)]) for d in (1, 2, 3)]
    new_image, spectrum = finish(parts, start, gt, flat)
    return new_image.reshape(image.shape), spectrum[0]


def solution(mesh):
    return jax.shard_map(
        local,
        mesh=mesh,
        in_specs=(
            P(("coil", "frame"), None, None, None, None),
            P("coil", None, None, None, None),
            P("coil", None, "frame", None, None, None),
            P("frame", None, None),
            P(),
        ),
        out_specs=(P(("coil", "frame"), None, None, None, None), P()),
        check_vma=False,
    )
```

profile of v0, /device:TPU:0, one launch (start us, length us, event | category | flops | bytes accessed | tf_op | source)
XLA Modules:
  0.0 105.6 jit_solution(8746473716875961863)
XLA Ops:
  0.6 0.0 copy-start
  0.6 0.0 copy-start.3
  0.7 2.2 %convert_element_type.3 = bf16[32,64,128]{2,1,0:T(8,128)(2,1)} convert(f32[32,64,128]{2,1,0:T(8,128)} %bitcast.8) | non-fusion elementwise | flops 262144 | bytes 1572864 | tf_op jit(solution)/shard_map/convert_element_type | solution.py:282
  2.8 8.4 %all-to-all-start = ((bf16[32,64,128]{2,1,0:T(8,128)(2,1)}), bf16[32,64,128]{2,1,0:T(8,128)(2,1)S(1)}, u32[]{:S(2)}, u32[]{:S(2)}) async-start(bf16[32,64,128]{2,1,0:T(8,128)(2,1)} %convert_element_type.3), calls=%async_computation | async-start | bytes 1048576 | tf_op jit(solution)/shard_map/all_to_all | solution.py:282
  11.2 2.0 %constant_dynamic-slice_fusion.1.refs_2_ = bf16[4,32,2,32,128]{4,3,2,1,0:T(8,128)(2,1)S(1)} fusion(bf16[4,128,2,32,128]{4,3,2,1,0:T(8,128)(2,1)} %refs_2_.7, s32[]{:T(128)S(6)} %select_n.4), kind=kLoop, calls=%fused_computation.1 | loop fusion | bytes 4194308 | tf_op jit(solution)/shard_map/dynamic_slice | solution.py:285
  13.3 3.4 %constant_dynamic-slice_fusion.refs_3_ = bf16[4,32,1,2,32,128]{5,4,3,2,1,0:T(8,128)(2,1)} fusion(bf16[4,128,1,2,32,128]{5,4,3,2,1,0:T(8,128)(2,1)} %refs_3_.7, s32[]{:T(128)S(6)} %select_n.4), kind=kLoop, calls=%fused_computation | loop fusion | bytes 4194308 | tf_op jit(solution)/shard_map/dynamic_slice | solution.py:285
  16.7 6.3 %all-to-all-done.refs_0_.refs_1_ = bf16[32,64,128]{2,1,0:T(8,128)(2,1)S(1)} async-done(((bf16[32,64,128]{2,1,0:T(8,128)(2,1)}), bf16[32,64,128]{2,1,0:T(8,128)(2,1)S(1)}, u32[]{:S(2)}, u32[]{:S(2)}) %all-to-all-start) | async-done | bytes 524320 | tf_op jit(solution)/shard_map/all_to_all | solution.py:282
  23.0 1.6 %collective-permute-start = (bf16[16,64,128]{2,1,0:T(8,128)(2,1)S(1)}, bf16[16,64,128]{2,1,0:T(8,128)(2,1)S(1)}, u32[]{:S(2)}, u32[]{:S(2)}) collective-permute-start(bf16[16,64,128]{2,1,0:T(8,128)(2,1)S(1)} %get-tuple-element.30), channel_id=1, source_target_pairs={{0,32},{32,64},{64,96},{96,0},{1,33},{33,65},{65,97},{97,1},{2,34}... | collective-permute-start | bytes 786440 | tf_op jit(solution)/shard_map/ppermute | solution.py:277
  24.6 0.0 slice-start
  24.6 0.0 slice-start.2
  24.6 0.0 slice-start.1
  24.6 0.0 slice-start.3
  24.6 1.8 %collective-permute-start.1 = (bf16[16,64,128]{2,1,0:T(8,128)(2,1)S(1)}, bf16[16,64,128]{2,1,0:T(8,128)(2,1)S(1)}, u32[]{:S(2)}, u32[]{:S(2)}) collective-permute-start(bf16[16,64,128]{2,1,0:T(8,128)(2,1)S(1)} %get-tuple-element.29), channel_id=1, source_target_pairs={{0,96},{32,0},{64,32},{96,64},{1,97},{33,1},{65,33},{97,65},{2,98}... | collective-permute-start | bytes 786440 | tf_op jit(solution)/shard_map/ppermute | solution.py:280
  26.4 0.0 copy-done
  26.4 0.0 copy-done.3
  26.4 0.0 copy-start.2
  26.4 2.4 %copy-done.2 = bf16[4,32,1,2,32,128]{5,4,3,2,1,0:T(8,128)(2,1)S(1)} copy-done((bf16[4,32,1,2,32,128]{5,4,3,2,1,0:T(8,128)(2,1)S(1)}, bf16[4,32,1,2,32,128]{5,4,3,2,1,0:T(8,128)(2,1)}, u32[]{:S(2)}) %copy-start.2) | copy-done | bytes 2097176
  28.8 3.3 %coil_gradient.5 = (bf16[16,64,128]{2,1,0:T(8,128)(2,1)S(1)}, bf16[16,64,128]{2,1,0:T(8,128)(2,1)S(1)}) custom-call(s32[1]{0:T(128)} %constant.8.clone.1.coil_ref, bf16[32,64,128]{2,1,0:T(8,128)(2,1)S(1)} %all-to-all-done.refs_0_.refs_1_, bf16[32,64,128]{2,1,0:T(8,128)(2,1)S(1)} %all-to-all-done.refs_0_.refs_1_, ...), custom_call_target="tpu_custom_call" | custom-call | flops 8589934592 | bytes 5120000 | tf_op jit(solution)/shard_map/coil_gradient/pallas_call | solution.py:114
  32.1 0.5 collective-permute-done.refs_0_
  32.6 0.1 collective-permute-done.1.refs_1_
  32.7 1.5 %collective-permute-start.2 = (bf16[16,64,128]{2,1,0:T(8,128)(2,1)S(1)}, bf16[16,64,128]{2,1,0:T(8,128)(2,1)S(1)}, u32[]{:S(2)}, u32[]{:S(2)}) collective-permute-start(bf16[16,64,128]{2,1,0:T(8,128)(2,1)S(1)} %collective-permute-done.refs_0_), channel_id=1, source_target_pairs={{0,32},{32,64},{64,96},{96,0},{1,33},{33,65},{65,97},{97,1},{2,34}... | collective-permute-start | bytes 786440 | tf_op jit(solution)/shard_map/ppermute | solution.py:277
  34.2 1.7 %collective-permute-start.3 = (bf16[16,64,128]{2,1,0:T(8,128)(2,1)S(1)}, bf16[16,64,128]{2,1,0:T(8,128)(2,1)S(1)}, u32[]{:S(2)}, u32[]{:S(2)}) collective-permute-start(bf16[16,64,128]{2,1,0:T(8,128)(2,1)S(1)} %collective-permute-done.1.refs_1_), channel_id=1, source_target_pairs={{0,96},{32,0},{64,32},{96,64},{1,97},{33,1},{65,33},{97,65},{2,98}... | collective-permute-start | bytes 786440 | tf_op jit(solution)/shard_map/ppermute | solution.py:280
  35.9 0.0 slice-done
  35.9 0.0 slice-done.2
  35.9 0.0 slice-done.1
  35.9 0.0 slice-done.3
  35.9 3.4 %coil_gradient.6 = (bf16[16,64,128]{2,1,0:T(8,128)(2,1)S(1)}, bf16[16,64,128]{2,1,0:T(8,128)(2,1)S(1)}) custom-call(s32[1]{0:T(128)} %bitcast.1.coil_ref, bf16[16,64,128]{2,1,0:T(8,128)(2,1)S(1)} %collective-permute-done.refs_0_, bf16[16,64,128]{2,1,0:T(8,128)(2,1)S(1)} %collective-permute-done.1.refs_1_, bf16[4,128,2,32,128]{4,3,2,1,0:T(8,128)(2,1)S(1)} %bitcast.5, ...), custom_call_target="tpu_custom_call" | custom-call | flops 4294967296 | bytes 5120000 | tf_op jit(solution)/shard_map/coil_gradient/pallas_call | solution.py:114
  39.3 0.3 collective-permute-start.4
  39.7 3.0 %collective-permute-start.5 = (bf16[16,64,128]{2,1,0:T(8,128)(2,1)S(1)}, bf16[16,64,128]{2,1,0:T(8,128)(2,1)S(1)}, u32[]{:S(2)}, u32[]{:S(2)}) collective-permute-start(bf16[16,64,128]{2,1,0:T(8,128)(2,1)S(1)} %get-tuple-element.30), channel_id=1, source_target_pairs={{0,96},{32,0},{64,32},{96,64},{1,97},{33,1},{65,33},{97,65},{2,98}... | collective-permute-start | bytes 786440 | tf_op jit(solution)/shard_map/ppermute | solution.py:280
  42.6 0.0 collective-permute-done.2.refs_0_
  42.6 1.5 %coil_gradient.7 = bf16[16,64,128]{2,1,0:T(8,128)(2,1)S(1)} custom-call(s32[1]{0:T(128)} %bitcast.1.coil_ref, bf16[16,64,128]{2,1,0:T(8,128)(2,1)S(1)} %collective-permute-done.2.refs_0_, bf16[4,128,2,32,128]{4,3,2,1,0:T(8,128)(2,1)S(1)} %bitcast.5, bf16[4,128,1,2,32,128]{5,4,3,2,1,0:T(8,128)(2,1)S(1)} %bitcast.7, s32[1,32,128]{2,1,0:T(8,128)S(1)} %copy-done.3, ...), custom_call_target="tpu_custom_call" | custom-call | flops 2147483648 | bytes 2560000 | tf_op jit(solution)/shard_map/coil_gradient/pallas_call | solution.py:114
  44.2 0.1 collective-permute-start.6
  44.3 0.0 collective-permute-done.3.refs_0_
  44.3 1.5 %coil_gradient.8 = bf16[16,64,128]{2,1,0:T(8,128)(2,1)S(1)} custom-call(s32[1]{0:T(128)} %bitcast.1.coil_ref, bf16[16,64,128]{2,1,0:T(8,128)(2,1)S(1)} %collective-permute-done.3.refs_0_, bf16[4,128,2,32,128]{4,3,2,1,0:T(8,128)(2,1)S(1)} %bitcast.5, bf16[4,128,1,2,32,128]{5,4,3,2,1,0:T(8,128)(2,1)S(1)} %bitcast.7, s32[1,32,128]{2,1,0:T(8,128)S(1)} %copy-done.3, ...), custom_call_target="tpu_custom_call" | custom-call | flops 2147483648 | bytes 2560000 | tf_op jit(solution)/shard_map/coil_gradient/pallas_call | solution.py:114
  45.8 3.3 %collective-permute-start.10 = (bf16[16,64,128]{2,1,0:T(8,128)(2,1)S(1)}, bf16[16,64,128]{2,1,0:T(8,128)(2,1)S(1)}, u32[]{:S(2)}, u32[]{:S(2)}) collective-permute-start(bf16[16,64,128]{2,1,0:T(8,128)(2,1)S(1)} %coil_gradient.8), channel_id=1, source_target_pairs={{0,96},{32,0},{64,32},{96,64},{1,97},{33,1},{65,33},{97,65},{2,98}... | collective-permute-start | bytes 786440 | tf_op jit(solution)/shard_map/ppermute | solution.py:280
  49.1 0.1 collective-permute-start.8
  49.2 0.0 collective-permute-done.4.refs_0_
  49.2 1.9 %collective-permute-start.9 = (bf16[16,64,128]{2,1,0:T(8,128)(2,1)S(1)}, bf16[16,64,128]{2,1,0:T(8,128)(2,1)S(1)}, u32[]{:S(2)}, u32[]{:S(2)}) collective-permute-start(bf16[16,64,128]{2,1,0:T(8,128)(2,1)S(1)} %get-tuple-element.34), channel_id=1, source_target_pairs={{0,32},{32,64},{64,96},{96,0},{1,33},{33,65},{65,97},{97,1},{2,34}... | collective-permute-start | bytes 786440 | tf_op jit(solution)/shard_map/ppermute | solution.py:277
  51.1 0.0 collective-permute-done.5.refs_1_
  51.1 3.4 %coil_gradient.9 = (bf16[16,64,128]{2,1,0:T(8,128)(2,1)S(1)}, bf16[16,64,128]{2,1,0:T(8,128)(2,1)S(1)}) custom-call(s32[1]{0:T(128)} %bitcast.1.coil_ref, bf16[16,64,128]{2,1,0:T(8,128)(2,1)S(1)} %collective-permute-done.4.refs_0_, bf16[16,64,128]{2,1,0:T(8,128)(2,1)S(1)} %collective-permute-done.5.refs_1_, bf16[4,128,2,32,128]{4,3,2,1,0:T(8,128)(2,1)S(1)} %bitcast.5, ...), custom_call_target="tpu_custom_call" | custom-call | flops 4294967296 | bytes 5120000 | tf_op jit(solution)/shard_map/coil_gradient/pallas_call | solution.py:114
  54.5 0.2 collective-permute-done.6.b
  54.7 0.1 pair_sum.2
  54.8 0.1 collective-permute-start.7
  54.8 1.0 collective-permute-done.10.b
  55.9 0.1 pair_sum.3
  55.9 3.8 %collective-permute-start.11 = (bf16[16,64,128]{2,1,0:T(8,128)(2,1)S(1)}, bf16[16,64,128]{2,1,0:T(8,128)(2,1)S(1)}, u32[]{:S(2)}, u32[]{:S(2)}) collective-permute-start(bf16[16,64,128]{2,1,0:T(8,128)(2,1)S(1)} %pair_sum.3), channel_id=1, source_target_pairs={{0,96},{32,0},{64,32},{96,64},{1,97},{33,1},{65,33},{97,65},{2,98}... | collective-permute-start | bytes 786440 | tf_op jit(solution)/shard_map/ppermute | solution.py:280
  59.7 1.3 %collective-permute-done.8.c0 = bf16[16,64,128]{2,1,0:T(8,128)(2,1)S(1)} collective-permute-done((bf16[16,64,128]{2,1,0:T(8,128)(2,1)S(1)}, bf16[16,64,128]{2,1,0:T(8,128)(2,1)S(1)}, u32[]{:S(2)}, u32[]{:S(2)}) %collective-permute-start.8) | collective-permute-done | bytes 262176 | tf_op jit(solution)/shard_map/ppermute | solution.py:280
  61.0 0.0 collective-permute-done.9.b1
  61.0 3.3 %collective-permute-done.7.b0 = bf16[16,64,128]{2,1,0:T(8,128)(2,1)S(1)} collective-permute-done((bf16[16,64,128]{2,1,0:T(8,128)(2,1)S(1)}, bf16[16,64,128]{2,1,0:T(8,128)(2,1)S(1)}, u32[]{:S(2)}, u32[]{:S(2)}) %collective-permute-start.7) | collective-permute-done | bytes 262176 | tf_op jit(solution)/shard_map/ppermute | solution.py:277
  64.3 0.0 collective-permute-done.11.c1
  64.3 0.2 join_sums.1
  64.5 16.2 %all_to_all.15.g_ref = bf16[32,64,128]{2,1,0:T(8,128)(2,1)S(1)} all-to-all(bf16[32,64,128]{2,1,0:T(8,128)(2,1)S(1)} %join_sums.1), channel_id=1, replica_groups=mesh['coil'=4,'frame'=32] {'frame'}, dimensions={0} | all-to-all | bytes 1048576 | tf_op jit(solution)/shard_map/all_to_all | solution.py:300
  80.7 1.1 %gram.1 = (bf16[32,64,128]{2,1,0:T(8,128)(2,1)S(1)}, f32[8,128]{1,0:T(8,128)S(1)}) custom-call(bf16[32,64,128]{2,1,0:T(8,128)(2,1)S(1)} %all_to_all.15.g_ref), custom_call_target="tpu_custom_call" | custom-call | tf_op jit(solution)/shard_map/gram/pallas_call | solution.py:193
  81.8 11.3 %all_to_all.16 = f32[32,8,128]{2,1,0:T(8,128)S(1)} all-to-all(f32[32,8,128]{2,1,0:T(8,128)S(1)} %broadcast_in_dim.2), channel_id=1, replica_groups=mesh['coil'=4,'frame'=32] {'frame'}, dimensions={0} | all-to-all | bytes 262144 | tf_op jit(solution)/shard_map/all_to_all | solution.py:302
  93.1 0.7 collective-permute-start.12
  93.8 4.0 %collective-permute-start.13 = (f32[8,128]{1,0:T(8,128)S(1)}, f32[8,128]{1,0:T(8,128)S(1)}, u32[]{:S(2)}, u32[]{:S(2)}) collective-permute-start(f32[8,128]{1,0:T(8,128)S(1)} %reduce_sum.9.q0), channel_id=1, source_target_pairs={{0,64},{32,96},{64,0},{96,32},{1,65},{33,97},{65,1},{97,33},{2,66}... | collective-permute-start | bytes 12296 | tf_op jit(solution)/shard_map/ppermute | solution.py:306
  97.8 0.0 collective-permute-start.14
  97.8 0.0 copy-done.4
  97.8 0.1 copy.13.start_ref
  97.9 0.0 collective-permute-done.12.q1
  97.9 1.5 %collective-permute-done.13.q2 = f32[8,128]{1,0:T(8,128)S(1)} collective-permute-done((f32[8,128]{1,0:T(8,128)S(1)}, f32[8,128]{1,0:T(8,128)S(1)}, u32[]{:S(2)}, u32[]{:S(2)}) %collective-permute-start.13) | collective-permute-done | bytes 4128 | tf_op jit(solution)/shard_map/ppermute | solution.py:306
  99.4 3.2 %collective-permute-done.14.q3 = f32[8,128]{1,0:T(8,128)S(1)} collective-permute-done((f32[8,128]{1,0:T(8,128)S(1)}, f32[8,128]{1,0:T(8,128)S(1)}, u32[]{:S(2)}, u32[]{:S(2)}) %collective-permute-start.14) | collective-permute-done | bytes 4128 | tf_op jit(solution)/shard_map/ppermute | solution.py:306
  102.6 0.0 copy-done.1
  102.6 3.0 %finish.1 = (f32[32,64,128]{2,1,0:T(8,128)}, f32[1,8]{1,0:T(1,128)}) custom-call(f32[8,128]{1,0:T(8,128)S(1)} %reduce_sum.9.q0, f32[8,128]{1,0:T(8,128)S(1)} %collective-permute-done.12.q1, f32[8,128]{1,0:T(8,128)S(1)} %collective-permute-done.13.q2, f32[8,128]{1,0:T(8,128)S(1)} %collective-permute-done.14.q3, f32[2,32,8]{2,1,0:T(8,128)S(1)} %copy.13.start_ref, ...), custom_call_target="tpu_custom_call" | custom-call | tf_op jit(solution)/shard_map/finish/pallas_call | solution.py:249
  (7 shorter events, 0.1 us)
Async XLA Ops:
  0.6 25.8 %copy-start = (bf16[4,256,256]{2,1,0:T(8,128)(2,1)S(1)}, bf16[4,256,256]{2,1,0:T(8,128)(2,1)}, u32[]{:S(2)}) copy-start(bf16[4,256,256]{2,1,0:T(8,128)(2,1)} %constant.20.clone.refs_5_.refs_4_) | copy-start | bytes 1572868
  0.6 25.8 %copy-start.3 = (s32[1,32,128]{2,1,0:T(8,128)S(1)}, s32[1,32,128]{2,1,0:T(8,128)}, u32[]{:S(2)}) copy-start(s32[1,32,128]{2,1,0:T(8,128)} %refs_4_.7) | copy-start | bytes 49156
  2.8 20.2 %all-to-all-start = ((bf16[32,64,128]{2,1,0:T(8,128)(2,1)}), bf16[32,64,128]{2,1,0:T(8,128)(2,1)S(1)}, u32[]{:S(2)}, u32[]{:S(2)}) async-start(bf16[32,64,128]{2,1,0:T(8,128)(2,1)} %convert_element_type.3), calls=%async_computation | async-start | bytes 1048576 | tf_op jit(solution)/shard_map/all_to_all | solution.py:282
  23.0 9.6 %collective-permute-start = (bf16[16,64,128]{2,1,0:T(8,128)(2,1)S(1)}, bf16[16,64,128]{2,1,0:T(8,128)(2,1)S(1)}, u32[]{:S(2)}, u32[]{:S(2)}) collective-permute-start(bf16[16,64,128]{2,1,0:T(8,128)(2,1)S(1)} %get-tuple-element.30), channel_id=1, source_target_pairs={{0,32},{32,64},{64,96},{96,0},{1,33},{33,65},{65,97},{97,1},{2,34}... | collective-permute-start | bytes 786440 | tf_op jit(solution)/shard_map/ppermute | solution.py:277
  24.6 11.3 %slice-start = ((s8[8388608]{0:T(1024)(128)(4,1)}), s8[4194304]{0:T(1024)(128)(4,1)S(1)}, s32[]{:S(2)}) async-start(s8[8388608]{0:T(1024)(128)(4,1)} %bitcast.4), calls=%async_computation.3 | async-start | bytes 8388608
  24.6 11.3 %slice-start.2 = ((s8[8388608]{0:T(1024)(128)(4,1)}), s8[4194304]{0:T(1024)(128)(4,1)S(1)}, s32[]{:S(2)}) async-start(s8[8388608]{0:T(1024)(128)(4,1)} %bitcast.6), calls=%async_computation.5 | async-start | bytes 8388608
  24.6 11.3 %slice-start.1 = ((s8[8388608]{0:T(1024)(128)(4,1)}), s8[4194304]{0:T(1024)(128)(4,1)S(1)}, s32[]{:S(2)}) async-start(s8[8388608]{0:T(1024)(128)(4,1)} %bitcast.4), calls=%async_computation.4 | async-start | bytes 8388608
  24.6 11.3 %slice-start.3 = ((s8[8388608]{0:T(1024)(128)(4,1)}), s8[4194304]{0:T(1024)(128)(4,1)S(1)}, s32[]{:S(2)}) async-start(s8[8388608]{0:T(1024)(128)(4,1)} %bitcast.6), calls=%async_computation.6 | async-start | bytes 8388608
  24.6 8.1 %collective-permute-start.1 = (bf16[16,64,128]{2,1,0:T(8,128)(2,1)S(1)}, bf16[16,64,128]{2,1,0:T(8,128)(2,1)S(1)}, u32[]{:S(2)}, u32[]{:S(2)}) collective-permute-start(bf16[16,64,128]{2,1,0:T(8,128)(2,1)S(1)} %get-tuple-element.29), channel_id=1, source_target_pairs={{0,96},{32,0},{64,32},{96,64},{1,97},{33,1},{65,33},{97,65},{2,98}... | collective-permute-start | bytes 786440 | tf_op jit(solution)/shard_map/ppermute | solution.py:280
  26.4 2.4 %copy-start.2 = (bf16[4,32,1,2,32,128]{5,4,3,2,1,0:T(8,128)(2,1)S(1)}, bf16[4,32,1,2,32,128]{5,4,3,2,1,0:T(8,128)(2,1)}, u32[]{:S(2)}) copy-start(bf16[4,32,1,2,32,128]{5,4,3,2,1,0:T(8,128)(2,1)} %constant_dynamic-slice_fusion.refs_3_) | copy-start | bytes 6291460
  32.7 10.0 %collective-permute-start.2 = (bf16[16,64,128]{2,1,0:T(8,128)(2,1)S(1)}, bf16[16,64,128]{2,1,0:T(8,128)(2,1)S(1)}, u32[]{:S(2)}, u32[]{:S(2)}) collective-permute-start(bf16[16,64,128]{2,1,0:T(8,128)(2,1)S(1)} %collective-permute-done.refs_0_), channel_id=1, source_target_pairs={{0,32},{32,64},{64,96},{96,0},{1,33},{33,65},{65,97},{97,1},{2,34}... | collective-permute-start | bytes 786440 | tf_op jit(solution)/shard_map/ppermute | solution.py:277
  34.2 10.1 %collective-permute-start.3 = (bf16[16,64,128]{2,1,0:T(8,128)(2,1)S(1)}, bf16[16,64,128]{2,1,0:T(8,128)(2,1)S(1)}, u32[]{:S(2)}, u32[]{:S(2)}) collective-permute-start(bf16[16,64,128]{2,1,0:T(8,128)(2,1)S(1)} %collective-permute-done.1.refs_1_), channel_id=1, source_target_pairs={{0,96},{32,0},{64,32},{96,64},{1,97},{33,1},{65,33},{97,65},{2,98}... | collective-permute-start | bytes 786440 | tf_op jit(solution)/shard_map/ppermute | solution.py:280
  39.3 9.8 %collective-permute-start.4 = (bf16[16,64,128]{2,1,0:T(8,128)(2,1)S(1)}, bf16[16,64,128]{2,1,0:T(8,128)(2,1)S(1)}, u32[]{:S(2)}, u32[]{:S(2)}) collective-permute-start(bf16[16,64,128]{2,1,0:T(8,128)(2,1)S(1)} %get-tuple-element.29), channel_id=1, source_target_pairs={{0,32},{32,64},{64,96},{96,0},{1,33},{33,65},{65,97},{97,1},{2,34}... | collective-permute-start | bytes 786440 | tf_op jit(solution)/shard_map/ppermute | solution.py:277
  39.7 11.4 %collective-permute-start.5 = (bf16[16,64,128]{2,1,0:T(8,128)(2,1)S(1)}, bf16[16,64,128]{2,1,0:T(8,128)(2,1)S(1)}, u32[]{:S(2)}, u32[]{:S(2)}) collective-permute-start(bf16[16,64,128]{2,1,0:T(8,128)(2,1)S(1)} %get-tuple-element.30), channel_id=1, source_target_pairs={{0,96},{32,0},{64,32},{96,64},{1,97},{33,1},{65,33},{97,65},{2,98}... | collective-permute-start | bytes 786440 | tf_op jit(solution)/shard_map/ppermute | solution.py:280
  44.2 10.5 %collective-permute-start.6 = (bf16[16,64,128]{2,1,0:T(8,128)(2,1)S(1)}, bf16[16,64,128]{2,1,0:T(8,128)(2,1)S(1)}, u32[]{:S(2)}, u32[]{:S(2)}) collective-permute-start(bf16[16,64,128]{2,1,0:T(8,128)(2,1)S(1)} %coil_gradient.7), channel_id=1, source_target_pairs={{0,32},{32,64},{64,96},{96,0},{1,33},{33,65},{65,97},{97,1},{2,34}... | collective-permute-start | bytes 786440 | tf_op jit(solution)/shard_map/ppermute | solution.py:277
  45.8 10.0 %collective-permute-start.10 = (bf16[16,64,128]{2,1,0:T(8,128)(2,1)S(1)}, bf16[16,64,128]{2,1,0:T(8,128)(2,1)S(1)}, u32[]{:S(2)}, u32[]{:S(2)}) collective-permute-start(bf16[16,64,128]{2,1,0:T(8,128)(2,1)S(1)} %coil_gradient.8), channel_id=1, source_target_pairs={{0,96},{32,0},{64,32},{96,64},{1,97},{33,1},{65,33},{97,65},{2,98}... | collective-permute-start | bytes 786440 | tf_op jit(solution)/shard_map/ppermute | solution.py:280
  49.1 11.9 %collective-permute-start.8 = (bf16[16,64,128]{2,1,0:T(8,128)(2,1)S(1)}, bf16[16,64,128]{2,1,0:T(8,128)(2,1)S(1)}, u32[]{:S(2)}, u32[]{:S(2)}) collective-permute-start(bf16[16,64,128]{2,1,0:T(8,128)(2,1)S(1)} %get-tuple-element.32), channel_id=1, source_target_pairs={{0,96},{32,0},{64,32},{96,64},{1,97},{33,1},{65,33},{97,65},{2,98}... | collective-permute-start | bytes 786440 | tf_op jit(solution)/shard_map/ppermute | solution.py:280
  49.2 48.7 %copy-start.4 = (f32[2,32,8]{1,2,0:T(8,128)S(1)}, f32[2,32,8]{1,2,0:T(8,128)}, u32[]{:S(2)}) copy-start(f32[2,32,8]{1,2,0:T(8,128)} %param.14) | copy-start | bytes 6148
  49.2 53.5 %copy-start.1 = (f32[1,32,2,32,128]{4,3,2,1,0:T(8,128)S(1)}, f32[1,32,2,32,128]{4,3,2,1,0:T(8,128)}, u32[]{:S(2)}) copy-start(f32[1,32,2,32,128]{4,3,2,1,0:T(8,128)} %param.10) | copy-start | bytes 3145732
  49.2 11.8 %collective-permute-start.9 = (bf16[16,64,128]{2,1,0:T(8,128)(2,1)S(1)}, bf16[16,64,128]{2,1,0:T(8,128)(2,1)S(1)}, u32[]{:S(2)}, u32[]{:S(2)}) collective-permute-start(bf16[16,64,128]{2,1,0:T(8,128)(2,1)S(1)} %get-tuple-element.34), channel_id=1, source_target_pairs={{0,32},{32,64},{64,96},{96,0},{1,33},{33,65},{65,97},{97,1},{2,34}... | collective-permute-start | bytes 786440 | tf_op jit(solution)/shard_map/ppermute | solution.py:277
  54.8 9.5 %collective-permute-start.7 = (bf16[16,64,128]{2,1,0:T(8,128)(2,1)S(1)}, bf16[16,64,128]{2,1,0:T(8,128)(2,1)S(1)}, u32[]{:S(2)}, u32[]{:S(2)}) collective-permute-start(bf16[16,64,128]{2,1,0:T(8,128)(2,1)S(1)} %pair_sum.2), channel_id=1, source_target_pairs={{0,32},{32,64},{64,96},{96,0},{1,33},{33,65},{65,97},{97,1},{2,34}... | collective-permute-start | bytes 786440 | tf_op jit(solution)/shard_map/ppermute | solution.py:277
  55.9 8.3 %collective-permute-start.11 = (bf16[16,64,128]{2,1,0:T(8,128)(2,1)S(1)}, bf16[16,64,128]{2,1,0:T(8,128)(2,1)S(1)}, u32[]{:S(2)}, u32[]{:S(2)}) collective-permute-start(bf16[16,64,128]{2,1,0:T(8,128)(2,1)S(1)} %pair_sum.3), channel_id=1, source_target_pairs={{0,96},{32,0},{64,32},{96,64},{1,97},{33,1},{65,33},{97,65},{2,98}... | collective-permute-start | bytes 786440 | tf_op jit(solution)/shard_map/ppermute | solution.py:280
  93.1 4.9 %collective-permute-start.12 = (f32[8,128]{1,0:T(8,128)S(1)}, f32[8,128]{1,0:T(8,128)S(1)}, u32[]{:S(2)}, u32[]{:S(2)}) collective-permute-start(f32[8,128]{1,0:T(8,128)S(1)} %reduce_sum.9.q0), channel_id=1, source_target_pairs={{0,32},{32,0},{64,96},{96,64},{1,33},{33,1},{65,97},{97,65},{2,34}... | collective-permute-start | bytes 12296 | tf_op jit(solution)/shard_map/ppermute | solution.py:306
  93.8 5.7 %collective-permute-start.13 = (f32[8,128]{1,0:T(8,128)S(1)}, f32[8,128]{1,0:T(8,128)S(1)}, u32[]{:S(2)}, u32[]{:S(2)}) collective-permute-start(f32[8,128]{1,0:T(8,128)S(1)} %reduce_sum.9.q0), channel_id=1, source_target_pairs={{0,64},{32,96},{64,0},{96,32},{1,65},{33,97},{65,1},{97,33},{2,66}... | collective-permute-start | bytes 12296 | tf_op jit(solution)/shard_map/ppermute | solution.py:306
  97.8 4.8 %collective-permute-start.14 = (f32[8,128]{1,0:T(8,128)S(1)}, f32[8,128]{1,0:T(8,128)S(1)}, u32[]{:S(2)}, u32[]{:S(2)}) collective-permute-start(f32[8,128]{1,0:T(8,128)S(1)} %reduce_sum.9.q0), channel_id=1, source_target_pairs={{0,96},{32,64},{64,32},{96,0},{1,97},{33,65},{65,33},{97,1},{2,98}... | collective-permute-start | bytes 12296 | tf_op jit(solution)/shard_map/ppermute | solution.py:306
where the time goes:
time: 106 us
  starting transfers between devices  32.3 us (30%)
  blocking collectives  27.5 us (26%)
  Pallas kernels  17.5 us (17%)
  waiting for transfers between devices  17.4 us (16%)
  local copies, waits for them, and re-layouts  7.93 us (7%)
  other arithmetic  2.2 us (2%)
    all_to_all x1, blocking collectives, local(): lax.all_to_all(gradient, 'frame', split_axis=0, concat_axis=0, tiled=True)  16.2 us
    ppermute x6, starting transfers between devices, left(): return lax.ppermute(x, 'coil', LEFT)  13.6 us
    pallas_call x5, Pallas kernels, coil_gradient(): pl.pallas_call(grad_kernel, grid_spec=pltpu.PrefetchScalarGridSpec(num_sc...  13.1 us
    all_to_all x1, blocking collectives, local(): lax.all_to_all(jnp.broadcast_to(q[None], (FRAMES, 8, 128)), 'frame', spli...  11.3 us
    all_to_all x1, starting transfers between devices, local(): lax.all_to_all(flat.astype(BF), 'frame', split_axis=0, concat_axis=0, til...  8.42 us
    all_to_all x1, waiting for transfers between devices, local(): lax.all_to_all(flat.astype(BF), 'frame', split_axis=0, concat_axis=0, til...  6.34 us
    ppermute x6, starting transfers between devices, right(): return lax.ppermute(x, 'coil', RIGHT)  5.49 us
    dynamic_slice x2, local copies, waits for them, and re-layouts, local(): lax.dynamic_slice_in_dim(x, coil[0] * 2 * HALF, 2 * HALF, axis=1)  5.41 us
  transfers between devices with their start and end apart: 16, of which 9 were waited for; matrix products, arithmetic and copies ran while one was open for 5% of the time, Pallas kernels for 13%

commit v1 on v0

--- a/solution.py
+++ b/solution.py
@@ -168,19 +168,15 @@
     )(*first, *second)
 
 
-def gram_kernel(g_ref, gt_ref, q_ref, wide):
-    wide[...] = g_ref[...].reshape(FRAMES * 2 * NZ, NY).astype(F32)
+def gram_kernel(g_ref, gt_ref, q_ref):
     total = jnp.zeros((2 * FRAMES, 2 * FRAMES), F32)
-    for z in range(0, NZ, 2):
-        pair = []
-        for d in (z, z + 1):
-            re = wide[pl.ds(d, FRAMES, stride=2 * NZ), :]
-            im = wide[pl.ds(NZ + d, FRAMES, stride=2 * NZ), :]
-            block = jnp.concatenate([re, im], axis=0).astype(BF)
-            gt_ref[d] = block
-            pair.append(block)
-        both = jnp.concatenate(pair, axis=1)
-        total += lax.dot_general(both, both, (((1,), (1,)), ((), ())), preferred_element_type=F32)
+    for z in range(0, NZ, 16):
+        parts = [g_ref[:, pl.ds(p * NZ + z, 16), :].astype(F32) for p in range(2)]
+        blocks = jnp.concatenate([jnp.swapaxes(x, 0, 1) for x in parts], axis=1).astype(BF)
+        gt_ref[pl.ds(z, 16)] = blocks
+        for d in range(0, 16, 2):
+            both = jnp.concatenate([blocks[d], blocks[d + 1]], axis=1)
+            total += lax.dot_general(both, both, (((1,), (1,)), ((), ())), preferred_element_type=F32)
     h_re = total[:FRAMES, :FRAMES] + total[FRAMES:, FRAMES:]
     h_im = total[:FRAMES, FRAMES:] - total[FRAMES:, :FRAMES]
     row = lax.broadcasted_iota(jnp.int32, (FRAMES, FRAMES), 0)
@@ -196,7 +192,6 @@
             jax.ShapeDtypeStruct((NZ, 2 * FRAMES, NY), BF),
             jax.ShapeDtypeStruct((8, 128), F32),
         ),
-        scratch_shapes=[pltpu.VMEM((FRAMES * 2 * NZ, NY), F32)],
         compiler_params=pltpu.CompilerParams(vmem_limit_bytes=32 * 2**20),
         name="gram",
     )(g)
@@ -208,7 +203,7 @@
     )
 
 
-def final_kernel(q0, q1, q2, q3, start_ref, gt_ref, image_ref, out_ref, spec_ref, wide):
+def final_kernel(q0, q1, q2, q3, start_ref, gt_ref, image_ref, out_ref, spec_ref):
     packed = (q0[...] + q1[...]) + (q2[...] + q3[...])
     q = jnp.concatenate([packed[:, 32 * j : 32 * j + 32] for j in range(4)], axis=0)
     qt = q.T
@@ -216,33 +211,36 @@
     col = lax.broadcasted_iota(jnp.int32, (FRAMES, FRAMES), 1)
     h_re = jnp.where(row <= col, q, qt)
     h_im = jnp.where(row > col, q, jnp.where(row < col, -qt, 0.0))
-    v_re, v_im = start_ref[0], start_ref[1]
-    w_re = exact(h_re, v_re) - exact(h_im, v_im)
-    w_im = exact(h_re, v_im) + exact(h_im, v_re)
-    length = jnp.sqrt(jnp.sum(w_re * w_re + w_im * w_im, axis=0, keepdims=True) + EPSILON)
-    v_re, v_im = w_re / length, w_im / length
-    w_re = exact(h_re, v_re) - exact(h_im, v_im)
-    w_im = exact(h_re, v_im) + exact(h_im, v_re)
-    power = jnp.maximum(jnp.sum(v_re * w_re + v_im * w_im, axis=0, keepdims=True), 0.0)
-    last = jnp.sum(w_re * w_re + w_im * w_im, axis=0, keepdims=True)
+    h = jnp.concatenate(
+        [jnp.concatenate([h_re, -h_im], axis=1), jnp.concatenate([h_im, h_re], axis=1)], axis=0
+    )
+    w = exact(h, jnp.concatenate([start_ref[0], start_ref[1]], axis=0))
+    v = w / jnp.sqrt(jnp.sum(w * w, axis=0, keepdims=True) + EPSILON)
+    w = exact(h, v)
+    power = jnp.maximum(jnp.sum(v * w, axis=0, keepdims=True), 0.0)
+    last = jnp.sum(w * w, axis=0, keepdims=True)
     spec_ref[...] = jnp.sqrt(last + EPSILON) / jnp.sqrt(power + EPSILON)
     total = jnp.sum(power, axis=1, keepdims=True)
     scale = 0.5 * math.sqrt(NX * NY * NZ * FRAMES) / jnp.sqrt(total)
-    lanes = ((1,), (1,))
-    t_re = (exact(v_re, v_re, lanes) + exact(v_im, v_im, lanes)) * scale
-    t_im = (exact(v_im, v_re, lanes) - exact(v_re, v_im, lanes)) * scale
+    t = exact(v, v, ((1,), (1,)))
+    t_re = (t[:FRAMES, :FRAMES] + t[FRAMES:, FRAMES:]) * scale
+    t_im = (t[FRAMES:, :FRAMES] - t[:FRAMES, FRAMES:]) * scale
     left = jnp.concatenate(
         [jnp.concatenate([t_re, t_im], axis=1), jnp.concatenate([-t_im, t_re], axis=1)], axis=0
     )
     high = left.astype(BF)
     low = (left - high.astype(F32)).astype(BF)
     left = jnp.concatenate([high, low], axis=1)
-    for z in range(NZ):
-        block = gt_ref[z]
-        update = jnp.dot(left, jnp.concatenate([block, block], axis=0), preferred_element_type=F32)
-        wide[pl.ds(z, FRAMES, stride=2 * NZ), :] = update[:FRAMES]
-        wide[pl.ds(NZ + z, FRAMES, stride=2 * NZ), :] = update[FRAMES:]
-    out_ref[...] = 0.5 * image_ref[...] - wide[...].reshape(FRAMES, 2 * NZ, NY)
+    for z in range(0, NZ, 8):
+        update = []
+        for d in range(z, z + 8, 2):
+            both = jnp.concatenate([gt_ref[d], gt_ref[d + 1]], axis=1)
+            both = jnp.dot(left, jnp.concatenate([both, both], axis=0), preferred_element_type=F32)
+            update += [both[:, :NY], both[:, NY:]]
+        update = jnp.swapaxes(jnp.stack(update, axis=0), 0, 1)
+        for p in range(2):
+            rows = pl.ds(p * NZ + z, 8)
+            out_ref[:, rows, :] = 0.5 * image_ref[:, rows, :] - update[p * FRAMES : (p + 1) * FRAMES]
 
 
 def finish(parts, start, gt, image):
@@ -252,7 +250,6 @@
             jax.ShapeDtypeStruct((FRAMES, 2 * NZ, NY), F32),
             jax.ShapeDtypeStruct((1, start.shape[2]), F32),
         ),
-        scratch_shapes=[pltpu.VMEM((FRAMES * 2 * NZ, NY), F32)],
         compiler_params=pltpu.CompilerParams(vmem_limit_bytes=32 * 2**20),
         name="finish",
     )(*parts, start, gt, image)

time: 106 us -> 105 us (level)
  no operation moved by 1% of the time
where the time goes in v1:
time: 105 us
  starting transfers between devices  32.3 us (31%)
  blocking collectives  27.5 us (26%)
  waiting for transfers between devices  17.4 us (17%)
  Pallas kernels  16.5 us (16%)
  local copies, waits for them, and re-layouts  7.92 us (8%)
  other arithmetic  2.2 us (2%)
    all_to_all x1, blocking collectives, local(): lax.all_to_all(gradient, 'frame', split_axis=0, concat_axis=0, tiled=True)  16.2 us
    ppermute x6, starting transfers between devices, left(): return lax.ppermute(x, 'coil', LEFT)  13.6 us
    pallas_call x5, Pallas kernels, coil_gradient(): pl.pallas_call(grad_kernel, grid_spec=pltpu.PrefetchScalarGridSpec(num_sc...  13.1 us
    all_to_all x1, blocking collectives, local(): lax.all_to_all(jnp.broadcast_to(q[None], (FRAMES, 8, 128)), 'frame', spli...  11.3 us
    all_to_all x1, starting transfers between devices, local(): lax.all_to_all(flat.astype(BF), 'frame', split_axis=0, concat_axis=0, til...  8.42 us
    all_to_all x1, waiting for transfers between devices, local(): lax.all_to_all(flat.astype(BF), 'frame', split_axis=0, concat_axis=0, til...  6.34 us
    ppermute x6, starting transfers between devices, right(): return lax.ppermute(x, 'coil', RIGHT)  5.49 us
    dynamic_slice x2, local copies, waits for them, and re-layouts, local(): lax.dynamic_slice_in_dim(x, coil[0] * 2 * HALF, 2 * HALF, axis=1)  5.41 us
  transfers between devices with their start and end apart: 16, of which 9 were waited for; matrix products, arithmetic and copies ran while one was open for 5% of the time, Pallas kernels for 13%

profile of v1, /device:TPU:0, one launch (start us, length us, event | category | flops | bytes accessed | tf_op | source)
XLA Modules:
  0.0 104.5 jit_solution(15187111853016328360)
XLA Ops:
  0.6 0.0 copy-start
  0.6 0.0 copy-start.3
  0.7 2.2 %convert_element_type.3 = bf16[32,64,128]{2,1,0:T(8,128)(2,1)} convert(f32[32,64,128]{2,1,0:T(8,128)} %bitcast.8) | non-fusion elementwise | flops 262144 | bytes 1572864 | tf_op jit(solution)/shard_map/convert_element_type | solution.py:279
  2.8 8.4 %all-to-all-start = ((bf16[32,64,128]{2,1,0:T(8,128)(2,1)}), bf16[32,64,128]{2,1,0:T(8,128)(2,1)S(1)}, u32[]{:S(2)}, u32[]{:S(2)}) async-start(bf16[32,64,128]{2,1,0:T(8,128)(2,1)} %convert_element_type.3), calls=%async_computation | async-start | bytes 1048576 | tf_op jit(solution)/shard_map/all_to_all | solution.py:279
  11.2 2.0 %constant_dynamic-slice_fusion.1.refs_2_ = bf16[4,32,2,32,128]{4,3,2,1,0:T(8,128)(2,1)S(1)} fusion(bf16[4,128,2,32,128]{4,3,2,1,0:T(8,128)(2,1)} %refs_2_.7, s32[]{:T(128)S(6)} %select_n.4), kind=kLoop, calls=%fused_computation.1 | loop fusion | bytes 4194308 | tf_op jit(solution)/shard_map/dynamic_slice | solution.py:282
  13.3 3.4 %constant_dynamic-slice_fusion.refs_3_ = bf16[4,32,1,2,32,128]{5,4,3,2,1,0:T(8,128)(2,1)} fusion(bf16[4,128,1,2,32,128]{5,4,3,2,1,0:T(8,128)(2,1)} %refs_3_.7, s32[]{:T(128)S(6)} %select_n.4), kind=kLoop, calls=%fused_computation | loop fusion | bytes 4194308 | tf_op jit(solution)/shard_map/dynamic_slice | solution.py:282
  16.7 6.3 %all-to-all-done.refs_0_.refs_1_ = bf16[32,64,128]{2,1,0:T(8,128)(2,1)S(1)} async-done(((bf16[32,64,128]{2,1,0:T(8,128)(2,1)}), bf16[32,64,128]{2,1,0:T(8,128)(2,1)S(1)}, u32[]{:S(2)}, u32[]{:S(2)}) %all-to-all-start) | async-done | bytes 524320 | tf_op jit(solution)/shard_map/all_to_all | solution.py:279
  23.0 1.6 %collective-permute-start = (bf16[16,64,128]{2,1,0:T(8,128)(2,1)S(1)}, bf16[16,64,128]{2,1,0:T(8,128)(2,1)S(1)}, u32[]{:S(2)}, u32[]{:S(2)}) collective-permute-start(bf16[16,64,128]{2,1,0:T(8,128)(2,1)S(1)} %get-tuple-element.30), channel_id=1, source_target_pairs={{0,32},{32,64},{64,96},{96,0},{1,33},{33,65},{65,97},{97,1},{2,34}... | collective-permute-start | bytes 786440 | tf_op jit(solution)/shard_map/ppermute | solution.py:274
  24.6 0.0 slice-start
  24.6 0.0 slice-start.2
  24.6 0.0 slice-start.1
  24.6 0.0 slice-start.3
  24.6 1.8 %collective-permute-start.1 = (bf16[16,64,128]{2,1,0:T(8,128)(2,1)S(1)}, bf16[16,64,128]{2,1,0:T(8,128)(2,1)S(1)}, u32[]{:S(2)}, u32[]{:S(2)}) collective-permute-start(bf16[16,64,128]{2,1,0:T(8,128)(2,1)S(1)} %get-tuple-element.29), channel_id=1, source_target_pairs={{0,96},{32,0},{64,32},{96,64},{1,97},{33,1},{65,33},{97,65},{2,98}... | collective-permute-start | bytes 786440 | tf_op jit(solution)/shard_map/ppermute | solution.py:277
  26.4 0.0 copy-done
  26.4 0.0 copy-done.3
  26.4 0.0 copy-start.2
  26.4 2.4 %copy-done.2 = bf16[4,32,1,2,32,128]{5,4,3,2,1,0:T(8,128)(2,1)S(1)} copy-done((bf16[4,32,1,2,32,128]{5,4,3,2,1,0:T(8,128)(2,1)S(1)}, bf16[4,32,1,2,32,128]{5,4,3,2,1,0:T(8,128)(2,1)}, u32[]{:S(2)}) %copy-start.2) | copy-done | bytes 2097176
  28.8 3.3 %coil_gradient.5 = (bf16[16,64,128]{2,1,0:T(8,128)(2,1)S(1)}, bf16[16,64,128]{2,1,0:T(8,128)(2,1)S(1)}) custom-call(s32[1]{0:T(128)} %constant.8.clone.1.coil_ref, bf16[32,64,128]{2,1,0:T(8,128)(2,1)S(1)} %all-to-all-done.refs_0_.refs_1_, bf16[32,64,128]{2,1,0:T(8,128)(2,1)S(1)} %all-to-all-done.refs_0_.refs_1_, ...), custom_call_target="tpu_custom_call" | custom-call | flops 8589934592 | bytes 5120000 | tf_op jit(solution)/shard_map/coil_gradient/pallas_call | solution.py:114
  32.1 0.5 collective-permute-done.refs_0_
  32.6 0.1 collective-permute-done.1.refs_1_
  32.7 1.5 %collective-permute-start.2 = (bf16[16,64,128]{2,1,0:T(8,128)(2,1)S(1)}, bf16[16,64,128]{2,1,0:T(8,128)(2,1)S(1)}, u32[]{:S(2)}, u32[]{:S(2)}) collective-permute-start(bf16[16,64,128]{2,1,0:T(8,128)(2,1)S(1)} %collective-permute-done.refs_0_), channel_id=1, source_target_pairs={{0,32},{32,64},{64,96},{96,0},{1,33},{33,65},{65,97},{97,1},{2,34}... | collective-permute-start | bytes 786440 | tf_op jit(solution)/shard_map/ppermute | solution.py:274
  34.2 1.7 %collective-permute-start.3 = (bf16[16,64,128]{2,1,0:T(8,128)(2,1)S(1)}, bf16[16,64,128]{2,1,0:T(8,128)(2,1)S(1)}, u32[]{:S(2)}, u32[]{:S(2)}) collective-permute-start(bf16[16,64,128]{2,1,0:T(8,128)(2,1)S(1)} %collective-permute-done.1.refs_1_), channel_id=1, source_target_pairs={{0,96},{32,0},{64,32},{96,64},{1,97},{33,1},{65,33},{97,65},{2,98}... | collective-permute-start | bytes 786440 | tf_op jit(solution)/shard_map/ppermute | solution.py:277
  35.9 0.0 slice-done
  35.9 0.0 slice-done.2
  35.9 0.0 slice-done.1
  35.9 0.0 slice-done.3
  35.9 3.4 %coil_gradient.6 = (bf16[16,64,128]{2,1,0:T(8,128)(2,1)S(1)}, bf16[16,64,128]{2,1,0:T(8,128)(2,1)S(1)}) custom-call(s32[1]{0:T(128)} %bitcast.1.coil_ref, bf16[16,64,128]{2,1,0:T(8,128)(2,1)S(1)} %collective-permute-done.refs_0_, bf16[16,64,128]{2,1,0:T(8,128)(2,1)S(1)} %collective-permute-done.1.refs_1_, bf16[4,128,2,32,128]{4,3,2,1,0:T(8,128)(2,1)S(1)} %bitcast.5, ...), custom_call_target="tpu_custom_call" | custom-call | flops 4294967296 | bytes 5120000 | tf_op jit(solution)/shard_map/coil_gradient/pallas_call | solution.py:114
  39.3 0.3 collective-permute-start.4
  39.7 3.0 %collective-permute-start.5 = (bf16[16,64,128]{2,1,0:T(8,128)(2,1)S(1)}, bf16[16,64,128]{2,1,0:T(8,128)(2,1)S(1)}, u32[]{:S(2)}, u32[]{:S(2)}) collective-permute-start(bf16[16,64,128]{2,1,0:T(8,128)(2,1)S(1)} %get-tuple-element.30), channel_id=1, source_target_pairs={{0,96},{32,0},{64,32},{96,64},{1,97},{33,1},{65,33},{97,65},{2,98}... | collective-permute-start | bytes 786440 | tf_op jit(solution)/shard_map/ppermute | solution.py:277
  42.6 0.0 collective-permute-done.2.refs_0_
  42.6 1.5 %coil_gradient.7 = bf16[16,64,128]{2,1,0:T(8,128)(2,1)S(1)} custom-call(s32[1]{0:T(128)} %bitcast.1.coil_ref, bf16[16,64,128]{2,1,0:T(8,128)(2,1)S(1)} %collective-permute-done.2.refs_0_, bf16[4,128,2,32,128]{4,3,2,1,0:T(8,128)(2,1)S(1)} %bitcast.5, bf16[4,128,1,2,32,128]{5,4,3,2,1,0:T(8,128)(2,1)S(1)} %bitcast.7, s32[1,32,128]{2,1,0:T(8,128)S(1)} %copy-done.3, ...), custom_call_target="tpu_custom_call" | custom-call | flops 2147483648 | bytes 2560000 | tf_op jit(solution)/shard_map/coil_gradient/pallas_call | solution.py:114
  44.2 0.1 collective-permute-start.6
  44.3 0.0 collective-permute-done.3.refs_0_
  44.3 1.5 %coil_gradient.8 = bf16[16,64,128]{2,1,0:T(8,128)(2,1)S(1)} custom-call(s32[1]{0:T(128)} %bitcast.1.coil_ref, bf16[16,64,128]{2,1,0:T(8,128)(2,1)S(1)} %collective-permute-done.3.refs_0_, bf16[4,128,2,32,128]{4,3,2,1,0:T(8,128)(2,1)S(1)} %bitcast.5, bf16[4,128,1,2,32,128]{5,4,3,2,1,0:T(8,128)(2,1)S(1)} %bitcast.7, s32[1,32,128]{2,1,0:T(8,128)S(1)} %copy-done.3, ...), custom_call_target="tpu_custom_call" | custom-call | flops 2147483648 | bytes 2560000 | tf_op jit(solution)/shard_map/coil_gradient/pallas_call | solution.py:114
  45.8 3.3 %collective-permute-start.10 = (bf16[16,64,128]{2,1,0:T(8,128)(2,1)S(1)}, bf16[16,64,128]{2,1,0:T(8,128)(2,1)S(1)}, u32[]{:S(2)}, u32[]{:S(2)}) collective-permute-start(bf16[16,64,128]{2,1,0:T(8,128)(2,1)S(1)} %coil_gradient.8), channel_id=1, source_target_pairs={{0,96},{32,0},{64,32},{96,64},{1,97},{33,1},{65,33},{97,65},{2,98}... | collective-permute-start | bytes 786440 | tf_op jit(solution)/shard_map/ppermute | solution.py:277
  49.1 0.1 collective-permute-start.8
  49.2 0.0 collective-permute-done.4.refs_0_
  49.2 1.9 %collective-permute-start.9 = (bf16[16,64,128]{2,1,0:T(8,128)(2,1)S(1)}, bf16[16,64,128]{2,1,0:T(8,128)(2,1)S(1)}, u32[]{:S(2)}, u32[]{:S(2)}) collective-permute-start(bf16[16,64,128]{2,1,0:T(8,128)(2,1)S(1)} %get-tuple-element.34), channel_id=1, source_target_pairs={{0,32},{32,64},{64,96},{96,0},{1,33},{33,65},{65,97},{97,1},{2,34}... | collective-permute-start | bytes 786440 | tf_op jit(solution)/shard_map/ppermute | solution.py:274
  51.1 0.0 collective-permute-done.5.refs_1_
  51.1 3.4 %coil_gradient.9 = (bf16[16,64,128]{2,1,0:T(8,128)(2,1)S(1)}, bf16[16,64,128]{2,1,0:T(8,128)(2,1)S(1)}) custom-call(s32[1]{0:T(128)} %bitcast.1.coil_ref, bf16[16,64,128]{2,1,0:T(8,128)(2,1)S(1)} %collective-permute-done.4.refs_0_, bf16[16,64,128]{2,1,0:T(8,128)(2,1)S(1)} %collective-permute-done.5.refs_1_, bf16[4,128,2,32,128]{4,3,2,1,0:T(8,128)(2,1)S(1)} %bitcast.5, ...), custom_call_target="tpu_custom_call" | custom-call | flops 4294967296 | bytes 5120000 | tf_op jit(solution)/shard_map/coil_gradient/pallas_call | solution.py:114
  54.5 0.2 collective-permute-done.6.b
  54.7 0.1 pair_sum.2
  54.8 0.1 collective-permute-start.7
  54.8 1.0 collective-permute-done.10.b
  55.9 0.1 pair_sum.3
  55.9 3.8 %collective-permute-start.11 = (bf16[16,64,128]{2,1,0:T(8,128)(2,1)S(1)}, bf16[16,64,128]{2,1,0:T(8,128)(2,1)S(1)}, u32[]{:S(2)}, u32[]{:S(2)}) collective-permute-start(bf16[16,64,128]{2,1,0:T(8,128)(2,1)S(1)} %pair_sum.3), channel_id=1, source_target_pairs={{0,96},{32,0},{64,32},{96,64},{1,97},{33,1},{65,33},{97,65},{2,98}... | collective-permute-start | bytes 786440 | tf_op jit(solution)/shard_map/ppermute | solution.py:277
  59.7 1.3 %collective-permute-done.8.c0 = bf16[16,64,128]{2,1,0:T(8,128)(2,1)S(1)} collective-permute-done((bf16[16,64,128]{2,1,0:T(8,128)(2,1)S(1)}, bf16[16,64,128]{2,1,0:T(8,128)(2,1)S(1)}, u32[]{:S(2)}, u32[]{:S(2)}) %collective-permute-start.8) | collective-permute-done | bytes 262176 | tf_op jit(solution)/shard_map/ppermute | solution.py:277
  61.0 0.0 collective-permute-done.9.b1
  61.0 3.3 %collective-permute-done.7.b0 = bf16[16,64,128]{2,1,0:T(8,128)(2,1)S(1)} collective-permute-done((bf16[16,64,128]{2,1,0:T(8,128)(2,1)S(1)}, bf16[16,64,128]{2,1,0:T(8,128)(2,1)S(1)}, u32[]{:S(2)}, u32[]{:S(2)}) %collective-permute-start.7) | collective-permute-done | bytes 262176 | tf_op jit(solution)/shard_map/ppermute | solution.py:274
  64.3 0.0 collective-permute-done.11.c1
  64.3 0.2 join_sums.1
  64.5 16.2 %all_to_all.15.g_ref = bf16[32,64,128]{2,1,0:T(8,128)(2,1)S(1)} all-to-all(bf16[32,64,128]{2,1,0:T(8,128)(2,1)S(1)} %join_sums.1), channel_id=1, replica_groups=mesh['coil'=4,'frame'=32] {'frame'}, dimensions={0} | all-to-all | bytes 1048576 | tf_op jit(solution)/shard_map/all_to_all | solution.py:297
  80.7 0.7 gram.1
  81.4 11.3 %all_to_all.16 = f32[32,8,128]{2,1,0:T(8,128)S(1)} all-to-all(f32[32,8,128]{2,1,0:T(8,128)S(1)} %broadcast_in_dim.2), channel_id=1, replica_groups=mesh['coil'=4,'frame'=32] {'frame'}, dimensions={0} | all-to-all | bytes 262144 | tf_op jit(solution)/shard_map/all_to_all | solution.py:299
  92.7 0.7 collective-permute-start.12
  93.4 4.0 %collective-permute-start.13 = (f32[8,128]{1,0:T(8,128)S(1)}, f32[8,128]{1,0:T(8,128)S(1)}, u32[]{:S(2)}, u32[]{:S(2)}) collective-permute-start(f32[8,128]{1,0:T(8,128)S(1)} %reduce_sum.9.q0), channel_id=1, source_target_pairs={{0,64},{32,96},{64,0},{96,32},{1,65},{33,97},{65,1},{97,33},{2,66}... | collective-permute-start | bytes 12296 | tf_op jit(solution)/shard_map/ppermute | solution.py:303
  97.4 0.0 collective-permute-start.14
  97.4 0.0 copy-done.4
  97.4 0.1 copy.13.start_ref
  97.5 0.0 collective-permute-done.12.q1
  97.5 1.5 %collective-permute-done.13.q2 = f32[8,128]{1,0:T(8,128)S(1)} collective-permute-done((f32[8,128]{1,0:T(8,128)S(1)}, f32[8,128]{1,0:T(8,128)S(1)}, u32[]{:S(2)}, u32[]{:S(2)}) %collective-permute-start.13) | collective-permute-done | bytes 4128 | tf_op jit(solution)/shard_map/ppermute | solution.py:303
  99.0 3.2 %collective-permute-done.14.q3 = f32[8,128]{1,0:T(8,128)S(1)} collective-permute-done((f32[8,128]{1,0:T(8,128)S(1)}, f32[8,128]{1,0:T(8,128)S(1)}, u32[]{:S(2)}, u32[]{:S(2)}) %collective-permute-start.14) | collective-permute-done | bytes 4128 | tf_op jit(solution)/shard_map/ppermute | solution.py:303
  102.2 0.0 copy-done.1
  102.2 2.3 %finish.1 = (f32[32,64,128]{2,1,0:T(8,128)}, f32[1,8]{1,0:T(1,128)}) custom-call(f32[8,128]{1,0:T(8,128)S(1)} %reduce_sum.9.q0, f32[8,128]{1,0:T(8,128)S(1)} %collective-permute-done.12.q1, f32[8,128]{1,0:T(8,128)S(1)} %collective-permute-done.13.q2, f32[8,128]{1,0:T(8,128)S(1)} %collective-permute-done.14.q3, f32[2,32,8]{2,1,0:T(8,128)S(1)} %copy.13.start_ref, ...), custom_call_target="tpu_custom_call" | custom-call | tf_op jit(solution)/shard_map/finish/pallas_call | solution.py:247
  (7 shorter events, 0.1 us)
Async XLA Ops:
  0.6 25.8 %copy-start = (bf16[4,256,256]{2,1,0:T(8,128)(2,1)S(1)}, bf16[4,256,256]{2,1,0:T(8,128)(2,1)}, u32[]{:S(2)}) copy-start(bf16[4,256,256]{2,1,0:T(8,128)(2,1)} %constant.20.clone.refs_5_.refs_4_) | copy-start | bytes 1572868
  0.6 25.8 %copy-start.3 = (s32[1,32,128]{2,1,0:T(8,128)S(1)}, s32[1,32,128]{2,1,0:T(8,128)}, u32[]{:S(2)}) copy-start(s32[1,32,128]{2,1,0:T(8,128)} %refs_4_.7) | copy-start | bytes 49156
  2.8 20.2 %all-to-all-start = ((bf16[32,64,128]{2,1,0:T(8,128)(2,1)}), bf16[32,64,128]{2,1,0:T(8,128)(2,1)S(1)}, u32[]{:S(2)}, u32[]{:S(2)}) async-start(bf16[32,64,128]{2,1,0:T(8,128)(2,1)} %convert_element_type.3), calls=%async_computation | async-start | bytes 1048576 | tf_op jit(solution)/shard_map/all_to_all | solution.py:279
  23.0 9.6 %collective-permute-start = (bf16[16,64,128]{2,1,0:T(8,128)(2,1)S(1)}, bf16[16,64,128]{2,1,0:T(8,128)(2,1)S(1)}, u32[]{:S(2)}, u32[]{:S(2)}) collective-permute-start(bf16[16,64,128]{2,1,0:T(8,128)(2,1)S(1)} %get-tuple-element.30), channel_id=1, source_target_pairs={{0,32},{32,64},{64,96},{96,0},{1,33},{33,65},{65,97},{97,1},{2,34}... | collective-permute-start | bytes 786440 | tf_op jit(solution)/shard_map/ppermute | solution.py:274
  24.6 11.3 %slice-start = ((s8[8388608]{0:T(1024)(128)(4,1)}), s8[4194304]{0:T(1024)(128)(4,1)S(1)}, s32[]{:S(2)}) async-start(s8[8388608]{0:T(1024)(128)(4,1)} %bitcast.4), calls=%async_computation.3 | async-start | bytes 8388608
  24.6 11.3 %slice-start.2 = ((s8[8388608]{0:T(1024)(128)(4,1)}), s8[4194304]{0:T(1024)(128)(4,1)S(1)}, s32[]{:S(2)}) async-start(s8[8388608]{0:T(1024)(128)(4,1)} %bitcast.6), calls=%async_computation.5 | async-start | bytes 8388608
  24.6 11.3 %slice-start.1 = ((s8[8388608]{0:T(1024)(128)(4,1)}), s8[4194304]{0:T(1024)(128)(4,1)S(1)}, s32[]{:S(2)}) async-start(s8[8388608]{0:T(1024)(128)(4,1)} %bitcast.4), calls=%async_computation.4 | async-start | bytes 8388608
  24.6 11.3 %slice-start.3 = ((s8[8388608]{0:T(1024)(128)(4,1)}), s8[4194304]{0:T(1024)(128)(4,1)S(1)}, s32[]{:S(2)}) async-start(s8[8388608]{0:T(1024)(128)(4,1)} %bitcast.6), calls=%async_computation.6 | async-start | bytes 8388608
  24.6 8.1 %collective-permute-start.1 = (bf16[16,64,128]{2,1,0:T(8,128)(2,1)S(1)}, bf16[16,64,128]{2,1,0:T(8,128)(2,1)S(1)}, u32[]{:S(2)}, u32[]{:S(2)}) collective-permute-start(bf16[16,64,128]{2,1,0:T(8,128)(2,1)S(1)} %get-tuple-element.29), channel_id=1, source_target_pairs={{0,96},{32,0},{64,32},{96,64},{1,97},{33,1},{65,33},{97,65},{2,98}... | collective-permute-start | bytes 786440 | tf_op jit(solution)/shard_map/ppermute | solution.py:277
  26.4 2.4 %copy-start.2 = (bf16[4,32,1,2,32,128]{5,4,3,2,1,0:T(8,128)(2,1)S(1)}, bf16[4,32,1,2,32,128]{5,4,3,2,1,0:T(8,128)(2,1)}, u32[]{:S(2)}) copy-start(bf16[4,32,1,2,32,128]{5,4,3,2,1,0:T(8,128)(2,1)} %constant_dynamic-slice_fusion.refs_3_) | copy-start | bytes 6291460
  32.7 10.0 %collective-permute-start.2 = (bf16[16,64,128]{2,1,0:T(8,128)(2,1)S(1)}, bf16[16,64,128]{2,1,0:T(8,128)(2,1)S(1)}, u32[]{:S(2)}, u32[]{:S(2)}) collective-permute-start(bf16[16,64,128]{2,1,0:T(8,128)(2,1)S(1)} %collective-permute-done.refs_0_), channel_id=1, source_target_pairs={{0,32},{32,64},{64,96},{96,0},{1,33},{33,65},{65,97},{97,1},{2,34}... | collective-permute-start | bytes 786440 | tf_op jit(solution)/shard_map/ppermute | solution.py:274
  34.2 10.1 %collective-permute-start.3 = (bf16[16,64,128]{2,1,0:T(8,128)(2,1)S(1)}, bf16[16,64,128]{2,1,0:T(8,128)(2,1)S(1)}, u32[]{:S(2)}, u32[]{:S(2)}) collective-permute-start(bf16[16,64,128]{2,1,0:T(8,128)(2,1)S(1)} %collective-permute-done.1.refs_1_), channel_id=1, source_target_pairs={{0,96},{32,0},{64,32},{96,64},{1,97},{33,1},{65,33},{97,65},{2,98}... | collective-permute-start | bytes 786440 | tf_op jit(solution)/shard_map/ppermute | solution.py:277
  39.3 9.8 %collective-permute-start.4 = (bf16[16,64,128]{2,1,0:T(8,128)(2,1)S(1)}, bf16[16,64,128]{2,1,0:T(8,128)(2,1)S(1)}, u32[]{:S(2)}, u32[]{:S(2)}) collective-permute-start(bf16[16,64,128]{2,1,0:T(8,128)(2,1)S(1)} %get-tuple-element.29), channel_id=1, source_target_pairs={{0,32},{32,64},{64,96},{96,0},{1,33},{33,65},{65,97},{97,1},{2,34}... | collective-permute-start | bytes 786440 | tf_op jit(solution)/shard_map/ppermute | solution.py:274
  39.7 11.4 %collective-permute-start.5 = (bf16[16,64,128]{2,1,0:T(8,128)(2,1)S(1)}, bf16[16,64,128]{2,1,0:T(8,128)(2,1)S(1)}, u32[]{:S(2)}, u32[]{:S(2)}) collective-permute-start(bf16[16,64,128]{2,1,0:T(8,128)(2,1)S(1)} %get-tuple-element.30), channel_id=1, source_target_pairs={{0,96},{32,0},{64,32},{96,64},{1,97},{33,1},{65,33},{97,65},{2,98}... | collective-permute-start | bytes 786440 | tf_op jit(solution)/shard_map/ppermute | solution.py:277
  44.2 10.5 %collective-permute-start.6 = (bf16[16,64,128]{2,1,0:T(8,128)(2,1)S(1)}, bf16[16,64,128]{2,1,0:T(8,128)(2,1)S(1)}, u32[]{:S(2)}, u32[]{:S(2)}) collective-permute-start(bf16[16,64,128]{2,1,0:T(8,128)(2,1)S(1)} %coil_gradient.7), channel_id=1, source_target_pairs={{0,32},{32,64},{64,96},{96,0},{1,33},{33,65},{65,97},{97,1},{2,34}... | collective-permute-start | bytes 786440 | tf_op jit(solution)/shard_map/ppermute | solution.py:274
  45.8 10.0 %collective-permute-start.10 = (bf16[16,64,128]{2,1,0:T(8,128)(2,1)S(1)}, bf16[16,64,128]{2,1,0:T(8,128)(2,1)S(1)}, u32[]{:S(2)}, u32[]{:S(2)}) collective-permute-start(bf16[16,64,128]{2,1,0:T(8,128)(2,1)S(1)} %coil_gradient.8), channel_id=1, source_target_pairs={{0,96},{32,0},{64,32},{96,64},{1,97},{33,1},{65,33},{97,65},{2,98}... | collective-permute-start | bytes 786440 | tf_op jit(solution)/shard_map/ppermute | solution.py:277
  49.1 11.9 %collective-permute-start.8 = (bf16[16,64,128]{2,1,0:T(8,128)(2,1)S(1)}, bf16[16,64,128]{2,1,0:T(8,128)(2,1)S(1)}, u32[]{:S(2)}, u32[]{:S(2)}) collective-permute-start(bf16[16,64,128]{2,1,0:T(8,128)(2,1)S(1)} %get-tuple-element.32), channel_id=1, source_target_pairs={{0,96},{32,0},{64,32},{96,64},{1,97},{33,1},{65,33},{97,65},{2,98}... | collective-permute-start | bytes 786440 | tf_op jit(solution)/shard_map/ppermute | solution.py:277
  49.2 48.3 %copy-start.4 = (f32[2,32,8]{1,2,0:T(8,128)S(1)}, f32[2,32,8]{1,2,0:T(8,128)}, u32[]{:S(2)}) copy-start(f32[2,32,8]{1,2,0:T(8,128)} %param.14) | copy-start | bytes 6148
  49.2 53.1 %copy-start.1 = (f32[1,32,2,32,128]{4,3,2,1,0:T(8,128)S(1)}, f32[1,32,2,32,128]{4,3,2,1,0:T(8,128)}, u32[]{:S(2)}) copy-start(f32[1,32,2,32,128]{4,3,2,1,0:T(8,128)} %param.10) | copy-start | bytes 3145732
  49.2 11.8 %collective-permute-start.9 = (bf16[16,64,128]{2,1,0:T(8,128)(2,1)S(1)}, bf16[16,64,128]{2,1,0:T(8,128)(2,1)S(1)}, u32[]{:S(2)}, u32[]{:S(2)}) collective-permute-start(bf16[16,64,128]{2,1,0:T(8,128)(2,1)S(1)} %get-tuple-element.34), channel_id=1, source_target_pairs={{0,32},{32,64},{64,96},{96,0},{1,33},{33,65},{65,97},{97,1},{2,34}... | collective-permute-start | bytes 786440 | tf_op jit(solution)/shard_map/ppermute | solution.py:274
  54.8 9.5 %collective-permute-start.7 = (bf16[16,64,128]{2,1,0:T(8,128)(2,1)S(1)}, bf16[16,64,128]{2,1,0:T(8,128)(2,1)S(1)}, u32[]{:S(2)}, u32[]{:S(2)}) collective-permute-start(bf16[16,64,128]{2,1,0:T(8,128)(2,1)S(1)} %pair_sum.2), channel_id=1, source_target_pairs={{0,32},{32,64},{64,96},{96,0},{1,33},{33,65},{65,97},{97,1},{2,34}... | collective-permute-start | bytes 786440 | tf_op jit(solution)/shard_map/ppermute | solution.py:274
  55.9 8.3 %collective-permute-start.11 = (bf16[16,64,128]{2,1,0:T(8,128)(2,1)S(1)}, bf16[16,64,128]{2,1,0:T(8,128)(2,1)S(1)}, u32[]{:S(2)}, u32[]{:S(2)}) collective-permute-start(bf16[16,64,128]{2,1,0:T(8,128)(2,1)S(1)} %pair_sum.3), channel_id=1, source_target_pairs={{0,96},{32,0},{64,32},{96,64},{1,97},{33,1},{65,33},{97,65},{2,98}... | collective-permute-start | bytes 786440 | tf_op jit(solution)/shard_map/ppermute | solution.py:277
  92.7 4.9 %collective-permute-start.12 = (f32[8,128]{1,0:T(8,128)S(1)}, f32[8,128]{1,0:T(8,128)S(1)}, u32[]{:S(2)}, u32[]{:S(2)}) collective-permute-start(f32[8,128]{1,0:T(8,128)S(1)} %reduce_sum.9.q0), channel_id=1, source_target_pairs={{0,32},{32,0},{64,96},{96,64},{1,33},{33,1},{65,97},{97,65},{2,34}... | collective-permute-start | bytes 12296 | tf_op jit(solution)/shard_map/ppermute | solution.py:303
  93.4 5.7 %collective-permute-start.13 = (f32[8,128]{1,0:T(8,128)S(1)}, f32[8,128]{1,0:T(8,128)S(1)}, u32[]{:S(2)}, u32[]{:S(2)}) collective-permute-start(f32[8,128]{1,0:T(8,128)S(1)} %reduce_sum.9.q0), channel_id=1, source_target_pairs={{0,64},{32,96},{64,0},{96,32},{1,65},{33,97},{65,1},{97,33},{2,66}... | collective-permute-start | bytes 12296 | tf_op jit(solution)/shard_map/ppermute | solution.py:303
  97.4 4.8 %collective-permute-start.14 = (f32[8,128]{1,0:T(8,128)S(1)}, f32[8,128]{1,0:T(8,128)S(1)}, u32[]{:S(2)}, u32[]{:S(2)}) collective-permute-start(f32[8,128]{1,0:T(8,128)S(1)} %reduce_sum.9.q0), channel_id=1, source_target_pairs={{0,96},{32,64},{64,32},{96,0},{1,97},{33,65},{65,33},{97,1},{2,98}... | collective-permute-start | bytes 12296 | tf_op jit(solution)/shard_map/ppermute | solution.py:303

commit v2 on v1

--- a/solution.py
+++ b/solution.py
@@ -204,7 +204,7 @@
 
 
 def final_kernel(q0, q1, q2, q3, start_ref, gt_ref, image_ref, out_ref, spec_ref):
-    packed = (q0[...] + q1[...]) + (q2[...] + q3[...])
+    packed = (q0[...] + q2[...]) + (q1[...] + q3[...])
     q = jnp.concatenate([packed[:, 32 * j : 32 * j + 32] for j in range(4)], axis=0)
     qt = q.T
     row = lax.broadcasted_iota(jnp.int32, (FRAMES, FRAMES), 0)
@@ -300,7 +300,8 @@
         jnp.broadcast_to(q[None], (FRAMES, 8, 128)), "frame", split_axis=0, concat_axis=0, tiled=True
     )
     q = jnp.sum(spread, axis=0)
-    parts = [q] + [lax.ppermute(q, "coil", [(i, i ^ d) for i in range(4)]) for d in (1, 2, 3)]
+    across = lax.ppermute(q, "coil", [(i, i ^ 2) for i in range(4)])
+    parts = [q, left(q), across, right(q)]
     new_image, spectrum = finish(parts, start, gt, flat)
     return new_image.reshape(image.shape), spectrum[0]
 

time: 105 us -> 104 us (level)
    ppermute x3 -> x1, starting transfers between devices: 4.77 us -> 0.01 us  [local(): across = lax.ppermute(q, 'coil', [(i, i ^ 2) for i in range(4)])]
    ppermute x6 -> x7, starting transfers between devices: 13.6 us -> 16.9 us  [left(): return lax.ppermute(x, 'coil', LEFT)]
    ppermute x6 -> x7, starting transfers between devices: 5.49 us -> 6.44 us  [right(): return lax.ppermute(x, 'coil', RIGHT)]
    ppermute x3 -> x1, waiting for transfers between devices: 4.72 us -> 3.78 us  [local(): across = lax.ppermute(q, 'coil', [(i, i ^ 2) for i in range(4)])]
    ppermute x6 -> x7, waiting for transfers between devices: 2.39 us -> 2.69 us  [left(): return lax.ppermute(x, 'coil', LEFT)]
    ppermute x6 -> x7, waiting for transfers between devices: 3.92 us -> 3.92 us  [right(): return lax.ppermute(x, 'coil', RIGHT)]
where the time goes in v2:
time: 104 us; the launch traced here: 103 us
  starting transfers between devices  31.8 us (31%)
  blocking collectives  27.5 us (26%)
  waiting for transfers between devices  16.7 us (16%)
  Pallas kernels  16.5 us (16%)
  local copies, waits for them, and re-layouts  7.92 us (8%)
  other arithmetic  2.2 us (2%)
    ppermute x7, starting transfers between devices, left(): return lax.ppermute(x, 'coil', LEFT)  16.9 us
    all_to_all x1, blocking collectives, local(): lax.all_to_all(gradient, 'frame', split_axis=0, concat_axis=0, tiled=True)  16.2 us
    pallas_call x5, Pallas kernels, coil_gradient(): pl.pallas_call(grad_kernel, grid_spec=pltpu.PrefetchScalarGridSpec(num_sc...  13.1 us
    all_to_all x1, blocking collectives, local(): lax.all_to_all(jnp.broadcast_to(q[None], (FRAMES, 8, 128)), 'frame', spli...  11.3 us
    all_to_all x1, starting transfers between devices, local(): lax.all_to_all(flat.astype(BF), 'frame', split_axis=0, concat_axis=0, til...  8.42 us
    ppermute x7, starting transfers between devices, right(): return lax.ppermute(x, 'coil', RIGHT)  6.44 us
    all_to_all x1, waiting for transfers between devices, local(): lax.all_to_all(flat.astype(BF), 'frame', split_axis=0, concat_axis=0, til...  6.34 us
    dynamic_slice x2, local copies, waits for them, and re-layouts, local(): lax.dynamic_slice_in_dim(x, coil[0] * 2 * HALF, 2 * HALF, axis=1)  5.41 us
  transfers between devices with their start and end apart: 16, of which 9 were waited for; matrix products, arithmetic and copies ran while one was open for 5% of the time, Pallas kernels for 13%

profile of v2, /device:TPU:0, one launch (start us, length us, event | category | flops | bytes accessed | tf_op | source)
XLA Modules:
  0.0 103.4 jit_solution(10014575013841630899)
XLA Ops:
  0.6 0.0 copy-start
  0.6 0.0 copy-start.3
  0.7 2.2 %convert_element_type.3 = bf16[32,64,128]{2,1,0:T(8,128)(2,1)} convert(f32[32,64,128]{2,1,0:T(8,128)} %bitcast.8) | non-fusion elementwise | flops 262144 | bytes 1572864 | tf_op jit(solution)/shard_map/convert_element_type | solution.py:279
  2.8 8.4 %all-to-all-start = ((bf16[32,64,128]{2,1,0:T(8,128)(2,1)}), bf16[32,64,128]{2,1,0:T(8,128)(2,1)S(1)}, u32[]{:S(2)}, u32[]{:S(2)}) async-start(bf16[32,64,128]{2,1,0:T(8,128)(2,1)} %convert_element_type.3), calls=%async_computation | async-start | bytes 1048576 | tf_op jit(solution)/shard_map/all_to_all | solution.py:279
  11.2 2.0 %constant_dynamic-slice_fusion.1.refs_2_ = bf16[4,32,2,32,128]{4,3,2,1,0:T(8,128)(2,1)S(1)} fusion(bf16[4,128,2,32,128]{4,3,2,1,0:T(8,128)(2,1)} %refs_2_.7, s32[]{:T(128)S(6)} %select_n.4), kind=kLoop, calls=%fused_computation.1 | loop fusion | bytes 4194308 | tf_op jit(solution)/shard_map/dynamic_slice | solution.py:282
  13.3 3.4 %constant_dynamic-slice_fusion.refs_3_ = bf16[4,32,1,2,32,128]{5,4,3,2,1,0:T(8,128)(2,1)} fusion(bf16[4,128,1,2,32,128]{5,4,3,2,1,0:T(8,128)(2,1)} %refs_3_.7, s32[]{:T(128)S(6)} %select_n.4), kind=kLoop, calls=%fused_computation | loop fusion | bytes 4194308 | tf_op jit(solution)/shard_map/dynamic_slice | solution.py:282
  16.7 6.3 %all-to-all-done.refs_0_.refs_1_ = bf16[32,64,128]{2,1,0:T(8,128)(2,1)S(1)} async-done(((bf16[32,64,128]{2,1,0:T(8,128)(2,1)}), bf16[32,64,128]{2,1,0:T(8,128)(2,1)S(1)}, u32[]{:S(2)}, u32[]{:S(2)}) %all-to-all-start) | async-done | bytes 524320 | tf_op jit(solution)/shard_map/all_to_all | solution.py:279
  23.0 1.6 %collective-permute-start = (bf16[16,64,128]{2,1,0:T(8,128)(2,1)S(1)}, bf16[16,64,128]{2,1,0:T(8,128)(2,1)S(1)}, u32[]{:S(2)}, u32[]{:S(2)}) collective-permute-start(bf16[16,64,128]{2,1,0:T(8,128)(2,1)S(1)} %get-tuple-element.30), channel_id=1, source_target_pairs={{0,32},{32,64},{64,96},{96,0},{1,33},{33,65},{65,97},{97,1},{2,34}... | collective-permute-start | bytes 786440 | tf_op jit(solution)/shard_map/ppermute | solution.py:274
  24.6 0.0 slice-start
  24.6 0.0 slice-start.2
  24.6 0.0 slice-start.1
  24.6 0.0 slice-start.3
  24.6 1.8 %collective-permute-start.1 = (bf16[16,64,128]{2,1,0:T(8,128)(2,1)S(1)}, bf16[16,64,128]{2,1,0:T(8,128)(2,1)S(1)}, u32[]{:S(2)}, u32[]{:S(2)}) collective-permute-start(bf16[16,64,128]{2,1,0:T(8,128)(2,1)S(1)} %get-tuple-element.29), channel_id=1, source_target_pairs={{0,96},{32,0},{64,32},{96,64},{1,97},{33,1},{65,33},{97,65},{2,98}... | collective-permute-start | bytes 786440 | tf_op jit(solution)/shard_map/ppermute | solution.py:277
  26.4 0.0 copy-done
  26.4 0.0 copy-done.3
  26.4 0.0 copy-start.2
  26.4 2.4 %copy-done.2 = bf16[4,32,1,2,32,128]{5,4,3,2,1,0:T(8,128)(2,1)S(1)} copy-done((bf16[4,32,1,2,32,128]{5,4,3,2,1,0:T(8,128)(2,1)S(1)}, bf16[4,32,1,2,32,128]{5,4,3,2,1,0:T(8,128)(2,1)}, u32[]{:S(2)}) %copy-start.2) | copy-done | bytes 2097176
  28.8 3.3 %coil_gradient.5 = (bf16[16,64,128]{2,1,0:T(8,128)(2,1)S(1)}, bf16[16,64,128]{2,1,0:T(8,128)(2,1)S(1)}) custom-call(s32[1]{0:T(128)} %constant.8.clone.1.coil_ref, bf16[32,64,128]{2,1,0:T(8,128)(2,1)S(1)} %all-to-all-done.refs_0_.refs_1_, bf16[32,64,128]{2,1,0:T(8,128)(2,1)S(1)} %all-to-all-done.refs_0_.refs_1_, ...), custom_call_target="tpu_custom_call" | custom-call | flops 8589934592 | bytes 5120000 | tf_op jit(solution)/shard_map/coil_gradient/pallas_call | solution.py:114
  32.1 0.5 collective-permute-done.refs_0_
  32.6 0.1 collective-permute-done.1.refs_1_
  32.7 1.5 %collective-permute-start.2 = (bf16[16,64,128]{2,1,0:T(8,128)(2,1)S(1)}, bf16[16,64,128]{2,1,0:T(8,128)(2,1)S(1)}, u32[]{:S(2)}, u32[]{:S(2)}) collective-permute-start(bf16[16,64,128]{2,1,0:T(8,128)(2,1)S(1)} %collective-permute-done.refs_0_), channel_id=1, source_target_pairs={{0,32},{32,64},{64,96},{96,0},{1,33},{33,65},{65,97},{97,1},{2,34}... | collective-permute-start | bytes 786440 | tf_op jit(solution)/shard_map/ppermute | solution.py:274
  34.2 1.7 %collective-permute-start.3 = (bf16[16,64,128]{2,1,0:T(8,128)(2,1)S(1)}, bf16[16,64,128]{2,1,0:T(8,128)(2,1)S(1)}, u32[]{:S(2)}, u32[]{:S(2)}) collective-permute-start(bf16[16,64,128]{2,1,0:T(8,128)(2,1)S(1)} %collective-permute-done.1.refs_1_), channel_id=1, source_target_pairs={{0,96},{32,0},{64,32},{96,64},{1,97},{33,1},{65,33},{97,65},{2,98}... | collective-permute-start | bytes 786440 | tf_op jit(solution)/shard_map/ppermute | solution.py:277
  35.9 0.0 slice-done
  35.9 0.0 slice-done.2
  35.9 0.0 slice-done.1
  35.9 0.0 slice-done.3
  35.9 3.4 %coil_gradient.6 = (bf16[16,64,128]{2,1,0:T(8,128)(2,1)S(1)}, bf16[16,64,128]{2,1,0:T(8,128)(2,1)S(1)}) custom-call(s32[1]{0:T(128)} %bitcast.1.coil_ref, bf16[16,64,128]{2,1,0:T(8,128)(2,1)S(1)} %collective-permute-done.refs_0_, bf16[16,64,128]{2,1,0:T(8,128)(2,1)S(1)} %collective-permute-done.1.refs_1_, bf16[4,128,2,32,128]{4,3,2,1,0:T(8,128)(2,1)S(1)} %bitcast.5, ...), custom_call_target="tpu_custom_call" | custom-call | flops 4294967296 | bytes 5120000 | tf_op jit(solution)/shard_map/coil_gradient/pallas_call | solution.py:114
  39.3 0.3 collective-permute-start.4
  39.7 3.0 %collective-permute-start.5 = (bf16[16,64,128]{2,1,0:T(8,128)(2,1)S(1)}, bf16[16,64,128]{2,1,0:T(8,128)(2,1)S(1)}, u32[]{:S(2)}, u32[]{:S(2)}) collective-permute-start(bf16[16,64,128]{2,1,0:T(8,128)(2,1)S(1)} %get-tuple-element.30), channel_id=1, source_target_pairs={{0,96},{32,0},{64,32},{96,64},{1,97},{33,1},{65,33},{97,65},{2,98}... | collective-permute-start | bytes 786440 | tf_op jit(solution)/shard_map/ppermute | solution.py:277
  42.6 0.0 collective-permute-done.2.refs_0_
  42.6 1.5 %coil_gradient.7 = bf16[16,64,128]{2,1,0:T(8,128)(2,1)S(1)} custom-call(s32[1]{0:T(128)} %bitcast.1.coil_ref, bf16[16,64,128]{2,1,0:T(8,128)(2,1)S(1)} %collective-permute-done.2.refs_0_, bf16[4,128,2,32,128]{4,3,2,1,0:T(8,128)(2,1)S(1)} %bitcast.5, bf16[4,128,1,2,32,128]{5,4,3,2,1,0:T(8,128)(2,1)S(1)} %bitcast.7, s32[1,32,128]{2,1,0:T(8,128)S(1)} %copy-done.3, ...), custom_call_target="tpu_custom_call" | custom-call | flops 2147483648 | bytes 2560000 | tf_op jit(solution)/shard_map/coil_gradient/pallas_call | solution.py:114
  44.2 0.1 collective-permute-start.6
  44.3 0.0 collective-permute-done.3.refs_0_
  44.3 1.5 %coil_gradient.8 = bf16[16,64,128]{2,1,0:T(8,128)(2,1)S(1)} custom-call(s32[1]{0:T(128)} %bitcast.1.coil_ref, bf16[16,64,128]{2,1,0:T(8,128)(2,1)S(1)} %collective-permute-done.3.refs_0_, bf16[4,128,2,32,128]{4,3,2,1,0:T(8,128)(2,1)S(1)} %bitcast.5, bf16[4,128,1,2,32,128]{5,4,3,2,1,0:T(8,128)(2,1)S(1)} %bitcast.7, s32[1,32,128]{2,1,0:T(8,128)S(1)} %copy-done.3, ...), custom_call_target="tpu_custom_call" | custom-call | flops 2147483648 | bytes 2560000 | tf_op jit(solution)/shard_map/coil_gradient/pallas_call | solution.py:114
  45.8 3.3 %collective-permute-start.10 = (bf16[16,64,128]{2,1,0:T(8,128)(2,1)S(1)}, bf16[16,64,128]{2,1,0:T(8,128)(2,1)S(1)}, u32[]{:S(2)}, u32[]{:S(2)}) collective-permute-start(bf16[16,64,128]{2,1,0:T(8,128)(2,1)S(1)} %coil_gradient.8), channel_id=1, source_target_pairs={{0,96},{32,0},{64,32},{96,64},{1,97},{33,1},{65,33},{97,65},{2,98}... | collective-permute-start | bytes 786440 | tf_op jit(solution)/shard_map/ppermute | solution.py:277
  49.1 0.1 collective-permute-start.8
  49.2 0.0 collective-permute-done.4.refs_0_
  49.2 1.9 %collective-permute-start.9 = (bf16[16,64,128]{2,1,0:T(8,128)(2,1)S(1)}, bf16[16,64,128]{2,1,0:T(8,128)(2,1)S(1)}, u32[]{:S(2)}, u32[]{:S(2)}) collective-permute-start(bf16[16,64,128]{2,1,0:T(8,128)(2,1)S(1)} %get-tuple-element.34), channel_id=1, source_target_pairs={{0,32},{32,64},{64,96},{96,0},{1,33},{33,65},{65,97},{97,1},{2,34}... | collective-permute-start | bytes 786440 | tf_op jit(solution)/shard_map/ppermute | solution.py:274
  51.1 0.0 collective-permute-done.5.refs_1_
  51.1 3.4 %coil_gradient.9 = (bf16[16,64,128]{2,1,0:T(8,128)(2,1)S(1)}, bf16[16,64,128]{2,1,0:T(8,128)(2,1)S(1)}) custom-call(s32[1]{0:T(128)} %bitcast.1.coil_ref, bf16[16,64,128]{2,1,0:T(8,128)(2,1)S(1)} %collective-permute-done.4.refs_0_, bf16[16,64,128]{2,1,0:T(8,128)(2,1)S(1)} %collective-permute-done.5.refs_1_, bf16[4,128,2,32,128]{4,3,2,1,0:T(8,128)(2,1)S(1)} %bitcast.5, ...), custom_call_target="tpu_custom_call" | custom-call | flops 4294967296 | bytes 5120000 | tf_op jit(solution)/shard_map/coil_gradient/pallas_call | solution.py:114
  54.5 0.2 collective-permute-done.6.b
  54.7 0.1 pair_sum.2
  54.8 0.1 collective-permute-start.7
  54.8 1.0 collective-permute-done.10.b
  55.9 0.1 pair_sum.3
  55.9 3.8 %collective-permute-start.11 = (bf16[16,64,128]{2,1,0:T(8,128)(2,1)S(1)}, bf16[16,64,128]{2,1,0:T(8,128)(2,1)S(1)}, u32[]{:S(2)}, u32[]{:S(2)}) collective-permute-start(bf16[16,64,128]{2,1,0:T(8,128)(2,1)S(1)} %pair_sum.3), channel_id=1, source_target_pairs={{0,96},{32,0},{64,32},{96,64},{1,97},{33,1},{65,33},{97,65},{2,98}... | collective-permute-start | bytes 786440 | tf_op jit(solution)/shard_map/ppermute | solution.py:277
  59.7 1.3 %collective-permute-done.8.c0 = bf16[16,64,128]{2,1,0:T(8,128)(2,1)S(1)} collective-permute-done((bf16[16,64,128]{2,1,0:T(8,128)(2,1)S(1)}, bf16[16,64,128]{2,1,0:T(8,128)(2,1)S(1)}, u32[]{:S(2)}, u32[]{:S(2)}) %collective-permute-start.8) | collective-permute-done | bytes 262176 | tf_op jit(solution)/shard_map/ppermute | solution.py:277
  61.0 0.0 collective-permute-done.9.b1
  61.0 3.3 %collective-permute-done.7.b0 = bf16[16,64,128]{2,1,0:T(8,128)(2,1)S(1)} collective-permute-done((bf16[16,64,128]{2,1,0:T(8,128)(2,1)S(1)}, bf16[16,64,128]{2,1,0:T(8,128)(2,1)S(1)}, u32[]{:S(2)}, u32[]{:S(2)}) %collective-permute-start.7) | collective-permute-done | bytes 262176 | tf_op jit(solution)/shard_map/ppermute | solution.py:274
  64.3 0.0 collective-permute-done.11.c1
  64.3 0.2 join_sums.1
  64.5 16.2 %all_to_all.15.g_ref = bf16[32,64,128]{2,1,0:T(8,128)(2,1)S(1)} all-to-all(bf16[32,64,128]{2,1,0:T(8,128)(2,1)S(1)} %join_sums.1), channel_id=1, replica_groups=mesh['coil'=4,'frame'=32] {'frame'}, dimensions={0} | all-to-all | bytes 1048576 | tf_op jit(solution)/shard_map/all_to_all | solution.py:297
  80.7 0.7 gram.1
  81.4 11.3 %all_to_all.16 = f32[32,8,128]{2,1,0:T(8,128)S(1)} all-to-all(f32[32,8,128]{2,1,0:T(8,128)S(1)} %broadcast_in_dim.2), channel_id=1, replica_groups=mesh['coil'=4,'frame'=32] {'frame'}, dimensions={0} | all-to-all | bytes 262144 | tf_op jit(solution)/shard_map/all_to_all | solution.py:299
  92.7 3.3 %collective-permute-start.12 = (f32[8,128]{1,0:T(8,128)S(1)}, f32[8,128]{1,0:T(8,128)S(1)}, u32[]{:S(2)}, u32[]{:S(2)}) collective-permute-start(f32[8,128]{1,0:T(8,128)S(1)} %reduce_sum.9.q0), channel_id=1, source_target_pairs={{0,96},{32,0},{64,32},{96,64},{1,97},{33,1},{65,33},{97,65},{2,98}... | collective-permute-start | bytes 12296 | tf_op jit(solution)/shard_map/ppermute | solution.py:277
  95.9 0.0 collective-permute-start.13
  95.9 0.9 collective-permute-start.14
  96.9 0.0 copy-done.4
  96.9 0.1 copy.13.start_ref
  97.0 0.3 collective-permute-done.12.q1
  97.3 3.8 %collective-permute-done.13.q2 = f32[8,128]{1,0:T(8,128)S(1)} collective-permute-done((f32[8,128]{1,0:T(8,128)S(1)}, f32[8,128]{1,0:T(8,128)S(1)}, u32[]{:S(2)}, u32[]{:S(2)}) %collective-permute-start.13) | collective-permute-done | bytes 4128 | tf_op jit(solution)/shard_map/ppermute | solution.py:303
  101.1 0.0 collective-permute-done.14.q3
  101.1 0.0 copy-done.1
  101.1 2.3 %finish.1 = (f32[32,64,128]{2,1,0:T(8,128)}, f32[1,8]{1,0:T(1,128)}) custom-call(f32[8,128]{1,0:T(8,128)S(1)} %reduce_sum.9.q0, f32[8,128]{1,0:T(8,128)S(1)} %collective-permute-done.12.q1, f32[8,128]{1,0:T(8,128)S(1)} %collective-permute-done.13.q2, f32[8,128]{1,0:T(8,128)S(1)} %collective-permute-done.14.q3, f32[2,32,8]{2,1,0:T(8,128)S(1)} %copy.13.start_ref, ...), custom_call_target="tpu_custom_call" | custom-call | tf_op jit(solution)/shard_map/finish/pallas_call | solution.py:247
  (7 shorter events, 0.1 us)
Async XLA Ops:
  0.6 25.8 %copy-start = (bf16[4,256,256]{2,1,0:T(8,128)(2,1)S(1)}, bf16[4,256,256]{2,1,0:T(8,128)(2,1)}, u32[]{:S(2)}) copy-start(bf16[4,256,256]{2,1,0:T(8,128)(2,1)} %constant.20.clone.refs_5_.refs_4_) | copy-start | bytes 1572868
  0.6 25.8 %copy-start.3 = (s32[1,32,128]{2,1,0:T(8,128)S(1)}, s32[1,32,128]{2,1,0:T(8,128)}, u32[]{:S(2)}) copy-start(s32[1,32,128]{2,1,0:T(8,128)} %refs_4_.7) | copy-start | bytes 49156
  2.8 20.2 %all-to-all-start = ((bf16[32,64,128]{2,1,0:T(8,128)(2,1)}), bf16[32,64,128]{2,1,0:T(8,128)(2,1)S(1)}, u32[]{:S(2)}, u32[]{:S(2)}) async-start(bf16[32,64,128]{2,1,0:T(8,128)(2,1)} %convert_element_type.3), calls=%async_computation | async-start | bytes 1048576 | tf_op jit(solution)/shard_map/all_to_all | solution.py:279
  23.0 9.6 %collective-permute-start = (bf16[16,64,128]{2,1,0:T(8,128)(2,1)S(1)}, bf16[16,64,128]{2,1,0:T(8,128)(2,1)S(1)}, u32[]{:S(2)}, u32[]{:S(2)}) collective-permute-start(bf16[16,64,128]{2,1,0:T(8,128)(2,1)S(1)} %get-tuple-element.30), channel_id=1, source_target_pairs={{0,32},{32,64},{64,96},{96,0},{1,33},{33,65},{65,97},{97,1},{2,34}... | collective-permute-start | bytes 786440 | tf_op jit(solution)/shard_map/ppermute | solution.py:274
  24.6 11.3 %slice-start = ((s8[8388608]{0:T(1024)(128)(4,1)}), s8[4194304]{0:T(1024)(128)(4,1)S(1)}, s32[]{:S(2)}) async-start(s8[8388608]{0:T(1024)(128)(4,1)} %bitcast.4), calls=%async_computation.3 | async-start | bytes 8388608
  24.6 11.3 %slice-start.2 = ((s8[8388608]{0:T(1024)(128)(4,1)}), s8[4194304]{0:T(1024)(128)(4,1)S(1)}, s32[]{:S(2)}) async-start(s8[8388608]{0:T(1024)(128)(4,1)} %bitcast.6), calls=%async_computation.5 | async-start | bytes 8388608
  24.6 11.3 %slice-start.1 = ((s8[8388608]{0:T(1024)(128)(4,1)}), s8[4194304]{0:T(1024)(128)(4,1)S(1)}, s32[]{:S(2)}) async-start(s8[8388608]{0:T(1024)(128)(4,1)} %bitcast.4), calls=%async_computation.4 | async-start | bytes 8388608
  24.6 11.3 %slice-start.3 = ((s8[8388608]{0:T(1024)(128)(4,1)}), s8[4194304]{0:T(1024)(128)(4,1)S(1)}, s32[]{:S(2)}) async-start(s8[8388608]{0:T(1024)(128)(4,1)} %bitcast.6), calls=%async_computation.6 | async-start | bytes 8388608
  24.6 8.1 %collective-permute-start.1 = (bf16[16,64,128]{2,1,0:T(8,128)(2,1)S(1)}, bf16[16,64,128]{2,1,0:T(8,128)(2,1)S(1)}, u32[]{:S(2)}, u32[]{:S(2)}) collective-permute-start(bf16[16,64,128]{2,1,0:T(8,128)(2,1)S(1)} %get-tuple-element.29), channel_id=1, source_target_pairs={{0,96},{32,0},{64,32},{96,64},{1,97},{33,1},{65,33},{97,65},{2,98}... | collective-permute-start | bytes 786440 | tf_op jit(solution)/shard_map/ppermute | solution.py:277
  26.4 2.4 %copy-start.2 = (bf16[4,32,1,2,32,128]{5,4,3,2,1,0:T(8,128)(2,1)S(1)}, bf16[4,32,1,2,32,128]{5,4,3,2,1,0:T(8,128)(2,1)}, u32[]{:S(2)}) copy-start(bf16[4,32,1,2,32,128]{5,4,3,2,1,0:T(8,128)(2,1)} %constant_dynamic-slice_fusion.refs_3_) | copy-start | bytes 6291460
  32.7 10.0 %collective-permute-start.2 = (bf16[16,64,128]{2,1,0:T(8,128)(2,1)S(1)}, bf16[16,64,128]{2,1,0:T(8,128)(2,1)S(1)}, u32[]{:S(2)}, u32[]{:S(2)}) collective-permute-start(bf16[16,64,128]{2,1,0:T(8,128)(2,1)S(1)} %collective-permute-done.refs_0_), channel_id=1, source_target_pairs={{0,32},{32,64},{64,96},{96,0},{1,33},{33,65},{65,97},{97,1},{2,34}... | collective-permute-start | bytes 786440 | tf_op jit(solution)/shard_map/ppermute | solution.py:274
  34.2 10.1 %collective-permute-start.3 = (bf16[16,64,128]{2,1,0:T(8,128)(2,1)S(1)}, bf16[16,64,128]{2,1,0:T(8,128)(2,1)S(1)}, u32[]{:S(2)}, u32[]{:S(2)}) collective-permute-start(bf16[16,64,128]{2,1,0:T(8,128)(2,1)S(1)} %collective-permute-done.1.refs_1_), channel_id=1, source_target_pairs={{0,96},{32,0},{64,32},{96,64},{1,97},{33,1},{65,33},{97,65},{2,98}... | collective-permute-start | bytes 786440 | tf_op jit(solution)/shard_map/ppermute | solution.py:277
  39.3 9.8 %collective-permute-start.4 = (bf16[16,64,128]{2,1,0:T(8,128)(2,1)S(1)}, bf16[16,64,128]{2,1,0:T(8,128)(2,1)S(1)}, u32[]{:S(2)}, u32[]{:S(2)}) collective-permute-start(bf16[16,64,128]{2,1,0:T(8,128)(2,1)S(1)} %get-tuple-element.29), channel_id=1, source_target_pairs={{0,32},{32,64},{64,96},{96,0},{1,33},{33,65},{65,97},{97,1},{2,34}... | collective-permute-start | bytes 786440 | tf_op jit(solution)/shard_map/ppermute | solution.py:274
  39.7 11.4 %collective-permute-start.5 = (bf16[16,64,128]{2,1,0:T(8,128)(2,1)S(1)}, bf16[16,64,128]{2,1,0:T(8,128)(2,1)S(1)}, u32[]{:S(2)}, u32[]{:S(2)}) collective-permute-start(bf16[16,64,128]{2,1,0:T(8,128)(2,1)S(1)} %get-tuple-element.30), channel_id=1, source_target_pairs={{0,96},{32,0},{64,32},{96,64},{1,97},{33,1},{65,33},{97,65},{2,98}... | collective-permute-start | bytes 786440 | tf_op jit(solution)/shard_map/ppermute | solution.py:277
  44.2 10.5 %collective-permute-start.6 = (bf16[16,64,128]{2,1,0:T(8,128)(2,1)S(1)}, bf16[16,64,128]{2,1,0:T(8,128)(2,1)S(1)}, u32[]{:S(2)}, u32[]{:S(2)}) collective-permute-start(bf16[16,64,128]{2,1,0:T(8,128)(2,1)S(1)} %coil_gradient.7), channel_id=1, source_target_pairs={{0,32},{32,64},{64,96},{96,0},{1,33},{33,65},{65,97},{97,1},{2,34}... | collective-permute-start | bytes 786440 | tf_op jit(solution)/shard_map/ppermute | solution.py:274
  45.8 10.0 %collective-permute-start.10 = (bf16[16,64,128]{2,1,0:T(8,128)(2,1)S(1)}, bf16[16,64,128]{2,1,0:T(8,128)(2,1)S(1)}, u32[]{:S(2)}, u32[]{:S(2)}) collective-permute-start(bf16[16,64,128]{2,1,0:T(8,128)(2,1)S(1)} %coil_gradient.8), channel_id=1, source_target_pairs={{0,96},{32,0},{64,32},{96,64},{1,97},{33,1},{65,33},{97,65},{2,98}... | collective-permute-start | bytes 786440 | tf_op jit(solution)/shard_map/ppermute | solution.py:277
  49.1 11.9 %collective-permute-start.8 = (bf16[16,64,128]{2,1,0:T(8,128)(2,1)S(1)}, bf16[16,64,128]{2,1,0:T(8,128)(2,1)S(1)}, u32[]{:S(2)}, u32[]{:S(2)}) collective-permute-start(bf16[16,64,128]{2,1,0:T(8,128)(2,1)S(1)} %get-tuple-element.32), channel_id=1, source_target_pairs={{0,96},{32,0},{64,32},{96,64},{1,97},{33,1},{65,33},{97,65},{2,98}... | collective-permute-start | bytes 786440 | tf_op jit(solution)/shard_map/ppermute | solution.py:277
  49.2 47.7 %copy-start.4 = (f32[2,32,8]{1,2,0:T(8,128)S(1)}, f32[2,32,8]{1,2,0:T(8,128)}, u32[]{:S(2)}) copy-start(f32[2,32,8]{1,2,0:T(8,128)} %param.14) | copy-start | bytes 6148
  49.2 51.9 %copy-start.1 = (f32[1,32,2,32,128]{4,3,2,1,0:T(8,128)S(1)}, f32[1,32,2,32,128]{4,3,2,1,0:T(8,128)}, u32[]{:S(2)}) copy-start(f32[1,32,2,32,128]{4,3,2,1,0:T(8,128)} %param.10) | copy-start | bytes 3145732
  49.2 11.8 %collective-permute-start.9 = (bf16[16,64,128]{2,1,0:T(8,128)(2,1)S(1)}, bf16[16,64,128]{2,1,0:T(8,128)(2,1)S(1)}, u32[]{:S(2)}, u32[]{:S(2)}) collective-permute-start(bf16[16,64,128]{2,1,0:T(8,128)(2,1)S(1)} %get-tuple-element.34), channel_id=1, source_target_pairs={{0,32},{32,64},{64,96},{96,0},{1,33},{33,65},{65,97},{97,1},{2,34}... | collective-permute-start | bytes 786440 | tf_op jit(solution)/shard_map/ppermute | solution.py:274
  54.8 9.5 %collective-permute-start.7 = (bf16[16,64,128]{2,1,0:T(8,128)(2,1)S(1)}, bf16[16,64,128]{2,1,0:T(8,128)(2,1)S(1)}, u32[]{:S(2)}, u32[]{:S(2)}) collective-permute-start(bf16[16,64,128]{2,1,0:T(8,128)(2,1)S(1)} %pair_sum.2), channel_id=1, source_target_pairs={{0,32},{32,64},{64,96},{96,0},{1,33},{33,65},{65,97},{97,1},{2,34}... | collective-permute-start | bytes 786440 | tf_op jit(solution)/shard_map/ppermute | solution.py:274
  55.9 8.3 %collective-permute-start.11 = (bf16[16,64,128]{2,1,0:T(8,128)(2,1)S(1)}, bf16[16,64,128]{2,1,0:T(8,128)(2,1)S(1)}, u32[]{:S(2)}, u32[]{:S(2)}) collective-permute-start(bf16[16,64,128]{2,1,0:T(8,128)(2,1)S(1)} %pair_sum.3), channel_id=1, source_target_pairs={{0,96},{32,0},{64,32},{96,64},{1,97},{33,1},{65,33},{97,65},{2,98}... | collective-permute-start | bytes 786440 | tf_op jit(solution)/shard_map/ppermute | solution.py:277
  92.7 4.6 %collective-permute-start.12 = (f32[8,128]{1,0:T(8,128)S(1)}, f32[8,128]{1,0:T(8,128)S(1)}, u32[]{:S(2)}, u32[]{:S(2)}) collective-permute-start(f32[8,128]{1,0:T(8,128)S(1)} %reduce_sum.9.q0), channel_id=1, source_target_pairs={{0,96},{32,0},{64,32},{96,64},{1,97},{33,1},{65,33},{97,65},{2,98}... | collective-permute-start | bytes 12296 | tf_op jit(solution)/shard_map/ppermute | solution.py:277
  95.9 5.1 %collective-permute-start.13 = (f32[8,128]{1,0:T(8,128)S(1)}, f32[8,128]{1,0:T(8,128)S(1)}, u32[]{:S(2)}, u32[]{:S(2)}) collective-permute-start(f32[8,128]{1,0:T(8,128)S(1)} %reduce_sum.9.q0), channel_id=1, source_target_pairs={{0,64},{32,96},{64,0},{96,32},{1,65},{33,97},{65,1},{97,33},{2,66}... | collective-permute-start | bytes 12296 | tf_op jit(solution)/shard_map/ppermute | solution.py:303
  95.9 5.1 %collective-permute-start.14 = (f32[8,128]{1,0:T(8,128)S(1)}, f32[8,128]{1,0:T(8,128)S(1)}, u32[]{:S(2)}, u32[]{:S(2)}) collective-permute-start(f32[8,128]{1,0:T(8,128)S(1)} %reduce_sum.9.q0), channel_id=1, source_target_pairs={{0,32},{32,64},{64,96},{96,0},{1,33},{33,65},{65,97},{97,1},{2,34}... | collective-permute-start | bytes 12296 | tf_op jit(solution)/shard_map/ppermute | solution.py:274

commit v3 on v2

--- a/solution.py
+++ b/solution.py
@@ -203,7 +203,7 @@
     )
 
 
-def final_kernel(q0, q1, q2, q3, start_ref, gt_ref, image_ref, out_ref, spec_ref):
+def final_kernel(q0, q1, q2, q3, start_ref, gt_ref, image_ref, out_ref, spec_ref, done, sems):
     packed = (q0[...] + q2[...]) + (q1[...] + q3[...])
     q = jnp.concatenate([packed[:, 32 * j : 32 * j + 32] for j in range(4)], axis=0)
     qt = q.T
@@ -231,6 +231,7 @@
     high = left.astype(BF)
     low = (left - high.astype(F32)).astype(BF)
     left = jnp.concatenate([high, low], axis=1)
+    copies = []
     for z in range(0, NZ, 8):
         update = []
         for d in range(z, z + 8, 2):
@@ -240,7 +241,13 @@
         update = jnp.swapaxes(jnp.stack(update, axis=0), 0, 1)
         for p in range(2):
             rows = pl.ds(p * NZ + z, 8)
-            out_ref[:, rows, :] = 0.5 * image_ref[:, rows, :] - update[p * FRAMES : (p + 1) * FRAMES]
+            done[:, rows, :] = 0.5 * image_ref[:, rows, :] - update[p * FRAMES : (p + 1) * FRAMES]
+            copies.append(
+                pltpu.make_async_copy(done.at[:, rows, :], out_ref.at[:, rows, :], sems.at[p, z // 8])
+            )
+            copies[-1].start()
+    for copy in copies:
+        copy.wait()
 
 
 def finish(parts, start, gt, image):
@@ -250,6 +257,11 @@
             jax.ShapeDtypeStruct((FRAMES, 2 * NZ, NY), F32),
             jax.ShapeDtypeStruct((1, start.shape[2]), F32),
         ),
+        out_specs=(pl.BlockSpec(memory_space=pl.ANY), pl.BlockSpec(memory_space=pltpu.VMEM)),
+        scratch_shapes=[
+            pltpu.VMEM((FRAMES, 2 * NZ, NY), F32),
+            pltpu.SemaphoreType.DMA((2, NZ // 8)),
+        ],
         compiler_params=pltpu.CompilerParams(vmem_limit_bytes=32 * 2**20),
         name="finish",
     )(*parts, start, gt, image)

time: 104 us -> 104 us (level)
  no operation moved by 1% of the time
where the time goes in v3:
time: 104 us
  starting transfers between devices  31.8 us (31%)
  blocking collectives  27.5 us (26%)
  Pallas kernels  16.8 us (16%)
  waiting for transfers between devices  16.7 us (16%)
  local copies, waits for them, and re-layouts  7.92 us (8%)
  other arithmetic  2.2 us (2%)
    ppermute x7, starting transfers between devices, left(): return lax.ppermute(x, 'coil', LEFT)  16.9 us
    all_to_all x1, blocking collectives, local(): lax.all_to_all(gradient, 'frame', split_axis=0, concat_axis=0, tiled=True)  16.2 us
    pallas_call x5, Pallas kernels, coil_gradient(): pl.pallas_call(grad_kernel, grid_spec=pltpu.PrefetchScalarGridSpec(num_sc...  13.1 us
    all_to_all x1, blocking collectives, local(): lax.all_to_all(jnp.broadcast_to(q[None], (FRAMES, 8, 128)), 'frame', spli...  11.3 us
    all_to_all x1, starting transfers between devices, local(): lax.all_to_all(flat.astype(BF), 'frame', split_axis=0, concat_axis=0, til...  8.42 us
    ppermute x7, starting transfers between devices, right(): return lax.ppermute(x, 'coil', RIGHT)  6.44 us
    all_to_all x1, waiting for transfers between devices, local(): lax.all_to_all(flat.astype(BF), 'frame', split_axis=0, concat_axis=0, til...  6.34 us
    dynamic_slice x2, local copies, waits for them, and re-layouts, local(): lax.dynamic_slice_in_dim(x, coil[0] * 2 * HALF, 2 * HALF, axis=1)  5.41 us
  transfers between devices with their start and end apart: 16, of which 9 were waited for; matrix products, arithmetic and copies ran while one was open for 5% of the time, Pallas kernels for 13%

profile of v3, /device:TPU:0, one launch (start us, length us, event | category | flops | bytes accessed | tf_op | source)
XLA Modules:
  0.0 103.9 jit_solution(14827951989071828868)
XLA Ops:
  0.6 0.0 copy-start
  0.6 0.0 copy-start.3
  0.7 2.2 %convert_element_type.3 = bf16[32,64,128]{2,1,0:T(8,128)(2,1)} convert(f32[32,64,128]{2,1,0:T(8,128)} %bitcast.8) | non-fusion elementwise | flops 262144 | bytes 1572864 | tf_op jit(solution)/shard_map/convert_element_type | solution.py:291
  2.8 8.4 %all-to-all-start = ((bf16[32,64,128]{2,1,0:T(8,128)(2,1)}), bf16[32,64,128]{2,1,0:T(8,128)(2,1)S(1)}, u32[]{:S(2)}, u32[]{:S(2)}) async-start(bf16[32,64,128]{2,1,0:T(8,128)(2,1)} %convert_element_type.3), calls=%async_computation | async-start | bytes 1048576 | tf_op jit(solution)/shard_map/all_to_all | solution.py:291
  11.2 2.0 %constant_dynamic-slice_fusion.1.refs_2_ = bf16[4,32,2,32,128]{4,3,2,1,0:T(8,128)(2,1)S(1)} fusion(bf16[4,128,2,32,128]{4,3,2,1,0:T(8,128)(2,1)} %refs_2_.7, s32[]{:T(128)S(6)} %select_n.4), kind=kLoop, calls=%fused_computation.1 | loop fusion | bytes 4194308 | tf_op jit(solution)/shard_map/dynamic_slice | solution.py:294
  13.3 3.4 %constant_dynamic-slice_fusion.refs_3_ = bf16[4,32,1,2,32,128]{5,4,3,2,1,0:T(8,128)(2,1)} fusion(bf16[4,128,1,2,32,128]{5,4,3,2,1,0:T(8,128)(2,1)} %refs_3_.7, s32[]{:T(128)S(6)} %select_n.4), kind=kLoop, calls=%fused_computation | loop fusion | bytes 4194308 | tf_op jit(solution)/shard_map/dynamic_slice | solution.py:294
  16.7 6.3 %all-to-all-done.refs_0_.refs_1_ = bf16[32,64,128]{2,1,0:T(8,128)(2,1)S(1)} async-done(((bf16[32,64,128]{2,1,0:T(8,128)(2,1)}), bf16[32,64,128]{2,1,0:T(8,128)(2,1)S(1)}, u32[]{:S(2)}, u32[]{:S(2)}) %all-to-all-start) | async-done | bytes 524320 | tf_op jit(solution)/shard_map/all_to_all | solution.py:291
  23.0 1.6 %collective-permute-start = (bf16[16,64,128]{2,1,0:T(8,128)(2,1)S(1)}, bf16[16,64,128]{2,1,0:T(8,128)(2,1)S(1)}, u32[]{:S(2)}, u32[]{:S(2)}) collective-permute-start(bf16[16,64,128]{2,1,0:T(8,128)(2,1)S(1)} %get-tuple-element.30), channel_id=1, source_target_pairs={{0,32},{32,64},{64,96},{96,0},{1,33},{33,65},{65,97},{97,1},{2,34}... | collective-permute-start | bytes 786440 | tf_op jit(solution)/shard_map/ppermute | solution.py:286
  24.6 0.0 slice-start
  24.6 0.0 slice-start.2
  24.6 0.0 slice-start.1
  24.6 0.0 slice-start.3
  24.6 1.8 %collective-permute-start.1 = (bf16[16,64,128]{2,1,0:T(8,128)(2,1)S(1)}, bf16[16,64,128]{2,1,0:T(8,128)(2,1)S(1)}, u32[]{:S(2)}, u32[]{:S(2)}) collective-permute-start(bf16[16,64,128]{2,1,0:T(8,128)(2,1)S(1)} %get-tuple-element.29), channel_id=1, source_target_pairs={{0,96},{32,0},{64,32},{96,64},{1,97},{33,1},{65,33},{97,65},{2,98}... | collective-permute-start | bytes 786440 | tf_op jit(solution)/shard_map/ppermute | solution.py:289
  26.4 0.0 copy-done
  26.4 0.0 copy-done.3
  26.4 2.4 %copy-done.2 = bf16[4,32,1,2,32,128]{5,4,3,2,1,0:T(8,128)(2,1)S(1)} copy-done((bf16[4,32,1,2,32,128]{5,4,3,2,1,0:T(8,128)(2,1)S(1)}, bf16[4,32,1,2,32,128]{5,4,3,2,1,0:T(8,128)(2,1)}, u32[]{:S(2)}) %copy-start.2) | copy-done | bytes 2097176
  28.8 3.3 %coil_gradient.5 = (bf16[16,64,128]{2,1,0:T(8,128)(2,1)S(1)}, bf16[16,64,128]{2,1,0:T(8,128)(2,1)S(1)}) custom-call(s32[1]{0:T(128)} %constant.8.clone.1.coil_ref, bf16[32,64,128]{2,1,0:T(8,128)(2,1)S(1)} %all-to-all-done.refs_0_.refs_1_, bf16[32,64,128]{2,1,0:T(8,128)(2,1)S(1)} %all-to-all-done.refs_0_.refs_1_, ...), custom_call_target="tpu_custom_call" | custom-call | flops 8589934592 | bytes 5120000 | tf_op jit(solution)/shard_map/coil_gradient/pallas_call | solution.py:114
  32.1 0.5 collective-permute-done.refs_0_
  32.6 0.1 collective-permute-done.1.refs_1_
  32.7 1.5 %collective-permute-start.2 = (bf16[16,64,128]{2,1,0:T(8,128)(2,1)S(1)}, bf16[16,64,128]{2,1,0:T(8,128)(2,1)S(1)}, u32[]{:S(2)}, u32[]{:S(2)}) collective-permute-start(bf16[16,64,128]{2,1,0:T(8,128)(2,1)S(1)} %collective-permute-done.refs_0_), channel_id=1, source_target_pairs={{0,32},{32,64},{64,96},{96,0},{1,33},{33,65},{65,97},{97,1},{2,34}... | collective-permute-start | bytes 786440 | tf_op jit(solution)/shard_map/ppermute | solution.py:286
  34.2 1.7 %collective-permute-start.3 = (bf16[16,64,128]{2,1,0:T(8,128)(2,1)S(1)}, bf16[16,64,128]{2,1,0:T(8,128)(2,1)S(1)}, u32[]{:S(2)}, u32[]{:S(2)}) collective-permute-start(bf16[16,64,128]{2,1,0:T(8,128)(2,1)S(1)} %collective-permute-done.1.refs_1_), channel_id=1, source_target_pairs={{0,96},{32,0},{64,32},{96,64},{1,97},{33,1},{65,33},{97,65},{2,98}... | collective-permute-start | bytes 786440 | tf_op jit(solution)/shard_map/ppermute | solution.py:289
  35.9 0.0 slice-done
  35.9 0.0 slice-done.2
  35.9 0.0 slice-done.1
  35.9 0.0 slice-done.3
  35.9 3.4 %coil_gradient.6 = (bf16[16,64,128]{2,1,0:T(8,128)(2,1)S(1)}, bf16[16,64,128]{2,1,0:T(8,128)(2,1)S(1)}) custom-call(s32[1]{0:T(128)} %bitcast.1.coil_ref, bf16[16,64,128]{2,1,0:T(8,128)(2,1)S(1)} %collective-permute-done.refs_0_, bf16[16,64,128]{2,1,0:T(8,128)(2,1)S(1)} %collective-permute-done.1.refs_1_, bf16[4,128,2,32,128]{4,3,2,1,0:T(8,128)(2,1)S(1)} %bitcast.5, ...), custom_call_target="tpu_custom_call" | custom-call | flops 4294967296 | bytes 5120000 | tf_op jit(solution)/shard_map/coil_gradient/pallas_call | solution.py:114
  39.3 0.3 collective-permute-start.4
  39.7 3.0 %collective-permute-start.5 = (bf16[16,64,128]{2,1,0:T(8,128)(2,1)S(1)}, bf16[16,64,128]{2,1,0:T(8,128)(2,1)S(1)}, u32[]{:S(2)}, u32[]{:S(2)}) collective-permute-start(bf16[16,64,128]{2,1,0:T(8,128)(2,1)S(1)} %get-tuple-element.30), channel_id=1, source_target_pairs={{0,96},{32,0},{64,32},{96,64},{1,97},{33,1},{65,33},{97,65},{2,98}... | collective-permute-start | bytes 786440 | tf_op jit(solution)/shard_map/ppermute | solution.py:289
  42.6 0.0 collective-permute-done.2.refs_0_
  42.6 1.5 %coil_gradient.7 = bf16[16,64,128]{2,1,0:T(8,128)(2,1)S(1)} custom-call(s32[1]{0:T(128)} %bitcast.1.coil_ref, bf16[16,64,128]{2,1,0:T(8,128)(2,1)S(1)} %collective-permute-done.2.refs_0_, bf16[4,128,2,32,128]{4,3,2,1,0:T(8,128)(2,1)S(1)} %bitcast.5, bf16[4,128,1,2,32,128]{5,4,3,2,1,0:T(8,128)(2,1)S(1)} %bitcast.7, s32[1,32,128]{2,1,0:T(8,128)S(1)} %copy-done.3, ...), custom_call_target="tpu_custom_call" | custom-call | flops 2147483648 | bytes 2560000 | tf_op jit(solution)/shard_map/coil_gradient/pallas_call | solution.py:114
  44.2 0.1 collective-permute-start.6
  44.3 0.0 collective-permute-done.3.refs_0_
  44.3 1.5 %coil_gradient.8 = bf16[16,64,128]{2,1,0:T(8,128)(2,1)S(1)} custom-call(s32[1]{0:T(128)} %bitcast.1.coil_ref, bf16[16,64,128]{2,1,0:T(8,128)(2,1)S(1)} %collective-permute-done.3.refs_0_, bf16[4,128,2,32,128]{4,3,2,1,0:T(8,128)(2,1)S(1)} %bitcast.5, bf16[4,128,1,2,32,128]{5,4,3,2,1,0:T(8,128)(2,1)S(1)} %bitcast.7, s32[1,32,128]{2,1,0:T(8,128)S(1)} %copy-done.3, ...), custom_call_target="tpu_custom_call" | custom-call | flops 2147483648 | bytes 2560000 | tf_op jit(solution)/shard_map/coil_gradient/pallas_call | solution.py:114
  45.8 3.3 %collective-permute-start.10 = (bf16[16,64,128]{2,1,0:T(8,128)(2,1)S(1)}, bf16[16,64,128]{2,1,0:T(8,128)(2,1)S(1)}, u32[]{:S(2)}, u32[]{:S(2)}) collective-permute-start(bf16[16,64,128]{2,1,0:T(8,128)(2,1)S(1)} %coil_gradient.8), channel_id=1, source_target_pairs={{0,96},{32,0},{64,32},{96,64},{1,97},{33,1},{65,33},{97,65},{2,98}... | collective-permute-start | bytes 786440 | tf_op jit(solution)/shard_map/ppermute | solution.py:289
  49.1 0.1 collective-permute-start.8
  49.2 0.0 copy-start.4
  49.2 0.0 collective-permute-done.4.refs_0_
  49.2 1.9 %collective-permute-start.9 = (bf16[16,64,128]{2,1,0:T(8,128)(2,1)S(1)}, bf16[16,64,128]{2,1,0:T(8,128)(2,1)S(1)}, u32[]{:S(2)}, u32[]{:S(2)}) collective-permute-start(bf16[16,64,128]{2,1,0:T(8,128)(2,1)S(1)} %get-tuple-element.34), channel_id=1, source_target_pairs={{0,32},{32,64},{64,96},{96,0},{1,33},{33,65},{65,97},{97,1},{2,34}... | collective-permute-start | bytes 786440 | tf_op jit(solution)/shard_map/ppermute | solution.py:286
  51.1 0.0 collective-permute-done.5.refs_1_
  51.1 3.4 %coil_gradient.9 = (bf16[16,64,128]{2,1,0:T(8,128)(2,1)S(1)}, bf16[16,64,128]{2,1,0:T(8,128)(2,1)S(1)}) custom-call(s32[1]{0:T(128)} %bitcast.1.coil_ref, bf16[16,64,128]{2,1,0:T(8,128)(2,1)S(1)} %collective-permute-done.4.refs_0_, bf16[16,64,128]{2,1,0:T(8,128)(2,1)S(1)} %collective-permute-done.5.refs_1_, bf16[4,128,2,32,128]{4,3,2,1,0:T(8,128)(2,1)S(1)} %bitcast.5, ...), custom_call_target="tpu_custom_call" | custom-call | flops 4294967296 | bytes 5120000 | tf_op jit(solution)/shard_map/coil_gradient/pallas_call | solution.py:114
  54.5 0.2 collective-permute-done.6.b
  54.7 0.1 pair_sum.2
  54.8 0.1 collective-permute-start.7
  54.8 1.0 collective-permute-done.10.b
  55.9 0.1 pair_sum.3
  55.9 3.8 %collective-permute-start.11 = (bf16[16,64,128]{2,1,0:T(8,128)(2,1)S(1)}, bf16[16,64,128]{2,1,0:T(8,128)(2,1)S(1)}, u32[]{:S(2)}, u32[]{:S(2)}) collective-permute-start(bf16[16,64,128]{2,1,0:T(8,128)(2,1)S(1)} %pair_sum.3), channel_id=1, source_target_pairs={{0,96},{32,0},{64,32},{96,64},{1,97},{33,1},{65,33},{97,65},{2,98}... | collective-permute-start | bytes 786440 | tf_op jit(solution)/shard_map/ppermute | solution.py:289
  59.7 1.3 %collective-permute-done.8.c0 = bf16[16,64,128]{2,1,0:T(8,128)(2,1)S(1)} collective-permute-done((bf16[16,64,128]{2,1,0:T(8,128)(2,1)S(1)}, bf16[16,64,128]{2,1,0:T(8,128)(2,1)S(1)}, u32[]{:S(2)}, u32[]{:S(2)}) %collective-permute-start.8) | collective-permute-done | bytes 262176 | tf_op jit(solution)/shard_map/ppermute | solution.py:289
  61.0 0.0 collective-permute-done.9.b1
  61.0 3.3 %collective-permute-done.7.b0 = bf16[16,64,128]{2,1,0:T(8,128)(2,1)S(1)} collective-permute-done((bf16[16,64,128]{2,1,0:T(8,128)(2,1)S(1)}, bf16[16,64,128]{2,1,0:T(8,128)(2,1)S(1)}, u32[]{:S(2)}, u32[]{:S(2)}) %collective-permute-start.7) | collective-permute-done | bytes 262176 | tf_op jit(solution)/shard_map/ppermute | solution.py:286
  64.3 0.0 collective-permute-done.11.c1
  64.3 0.2 join_sums.1
  64.5 16.2 %all_to_all.15.g_ref = bf16[32,64,128]{2,1,0:T(8,128)(2,1)S(1)} all-to-all(bf16[32,64,128]{2,1,0:T(8,128)(2,1)S(1)} %join_sums.1), channel_id=1, replica_groups=mesh['coil'=4,'frame'=32] {'frame'}, dimensions={0} | all-to-all | bytes 1048576 | tf_op jit(solution)/shard_map/all_to_all | solution.py:309
  80.7 0.7 gram.1
  81.4 11.3 %all_to_all.16 = f32[32,8,128]{2,1,0:T(8,128)S(1)} all-to-all(f32[32,8,128]{2,1,0:T(8,128)S(1)} %broadcast_in_dim.2), channel_id=1, replica_groups=mesh['coil'=4,'frame'=32] {'frame'}, dimensions={0} | all-to-all | bytes 262144 | tf_op jit(solution)/shard_map/all_to_all | solution.py:311
  92.7 3.3 %collective-permute-start.12 = (f32[8,128]{1,0:T(8,128)S(1)}, f32[8,128]{1,0:T(8,128)S(1)}, u32[]{:S(2)}, u32[]{:S(2)}) collective-permute-start(f32[8,128]{1,0:T(8,128)S(1)} %reduce_sum.9.q0), channel_id=1, source_target_pairs={{0,96},{32,0},{64,32},{96,64},{1,97},{33,1},{65,33},{97,65},{2,98}... | collective-permute-start | bytes 12296 | tf_op jit(solution)/shard_map/ppermute | solution.py:289
  95.9 0.0 collective-permute-start.13
  95.9 0.9 collective-permute-start.14
  96.9 0.0 copy-done.4
  96.9 0.1 copy.13.start_ref
  97.0 0.3 collective-permute-done.12.q1
  97.3 3.8 %collective-permute-done.13.q2 = f32[8,128]{1,0:T(8,128)S(1)} collective-permute-done((f32[8,128]{1,0:T(8,128)S(1)}, f32[8,128]{1,0:T(8,128)S(1)}, u32[]{:S(2)}, u32[]{:S(2)}) %collective-permute-start.13) | collective-permute-done | bytes 4128 | tf_op jit(solution)/shard_map/ppermute | solution.py:315
  101.1 0.0 collective-permute-done.14.q3
  101.1 0.0 copy-done.1
  101.1 2.6 %finish.1 = (f32[32,64,128]{2,1,0:T(8,128)}, f32[1,8]{1,0:T(1,128)}) custom-call(f32[8,128]{1,0:T(8,128)S(1)} %reduce_sum.9.q0, f32[8,128]{1,0:T(8,128)S(1)} %collective-permute-done.12.q1, f32[8,128]{1,0:T(8,128)S(1)} %collective-permute-done.13.q2, f32[8,128]{1,0:T(8,128)S(1)} %collective-permute-done.14.q3, f32[2,32,8]{2,1,0:T(8,128)S(1)} %copy.13.start_ref, ...), custom_call_target="tpu_custom_call" | custom-call | tf_op jit(solution)/shard_map/finish/pallas_call | solution.py:254
  (7 shorter events, 0.1 us)
Async XLA Ops:
  0.6 25.8 %copy-start = (bf16[4,256,256]{2,1,0:T(8,128)(2,1)S(1)}, bf16[4,256,256]{2,1,0:T(8,128)(2,1)}, u32[]{:S(2)}) copy-start(bf16[4,256,256]{2,1,0:T(8,128)(2,1)} %constant.20.clone.refs_5_.refs_4_) | copy-start | bytes 1572868
  0.6 25.8 %copy-start.3 = (s32[1,32,128]{2,1,0:T(8,128)S(1)}, s32[1,32,128]{2,1,0:T(8,128)}, u32[]{:S(2)}) copy-start(s32[1,32,128]{2,1,0:T(8,128)} %refs_4_.7) | copy-start | bytes 49156
  2.8 20.2 %all-to-all-start = ((bf16[32,64,128]{2,1,0:T(8,128)(2,1)}), bf16[32,64,128]{2,1,0:T(8,128)(2,1)S(1)}, u32[]{:S(2)}, u32[]{:S(2)}) async-start(bf16[32,64,128]{2,1,0:T(8,128)(2,1)} %convert_element_type.3), calls=%async_computation | async-start | bytes 1048576 | tf_op jit(solution)/shard_map/all_to_all | solution.py:291
  23.0 9.6 %collective-permute-start = (bf16[16,64,128]{2,1,0:T(8,128)(2,1)S(1)}, bf16[16,64,128]{2,1,0:T(8,128)(2,1)S(1)}, u32[]{:S(2)}, u32[]{:S(2)}) collective-permute-start(bf16[16,64,128]{2,1,0:T(8,128)(2,1)S(1)} %get-tuple-element.30), channel_id=1, source_target_pairs={{0,32},{32,64},{64,96},{96,0},{1,33},{33,65},{65,97},{97,1},{2,34}... | collective-permute-start | bytes 786440 | tf_op jit(solution)/shard_map/ppermute | solution.py:286
  24.6 11.3 %slice-start = ((s8[8388608]{0:T(1024)(128)(4,1)}), s8[4194304]{0:T(1024)(128)(4,1)S(1)}, s32[]{:S(2)}) async-start(s8[8388608]{0:T(1024)(128)(4,1)} %bitcast.4), calls=%async_computation.3 | async-start | bytes 8388608
  24.6 11.3 %slice-start.2 = ((s8[8388608]{0:T(1024)(128)(4,1)}), s8[4194304]{0:T(1024)(128)(4,1)S(1)}, s32[]{:S(2)}) async-start(s8[8388608]{0:T(1024)(128)(4,1)} %bitcast.6), calls=%async_computation.5 | async-start | bytes 8388608
  24.6 11.3 %slice-start.1 = ((s8[8388608]{0:T(1024)(128)(4,1)}), s8[4194304]{0:T(1024)(128)(4,1)S(1)}, s32[]{:S(2)}) async-start(s8[8388608]{0:T(1024)(128)(4,1)} %bitcast.4), calls=%async_computation.4 | async-start | bytes 8388608
  24.6 11.3 %slice-start.3 = ((s8[8388608]{0:T(1024)(128)(4,1)}), s8[4194304]{0:T(1024)(128)(4,1)S(1)}, s32[]{:S(2)}) async-start(s8[8388608]{0:T(1024)(128)(4,1)} %bitcast.6), calls=%async_computation.6 | async-start | bytes 8388608
  24.6 8.1 %collective-permute-start.1 = (bf16[16,64,128]{2,1,0:T(8,128)(2,1)S(1)}, bf16[16,64,128]{2,1,0:T(8,128)(2,1)S(1)}, u32[]{:S(2)}, u32[]{:S(2)}) collective-permute-start(bf16[16,64,128]{2,1,0:T(8,128)(2,1)S(1)} %get-tuple-element.29), channel_id=1, source_target_pairs={{0,96},{32,0},{64,32},{96,64},{1,97},{33,1},{65,33},{97,65},{2,98}... | collective-permute-start | bytes 786440 | tf_op jit(solution)/shard_map/ppermute | solution.py:289
  26.4 2.4 %copy-start.2 = (bf16[4,32,1,2,32,128]{5,4,3,2,1,0:T(8,128)(2,1)S(1)}, bf16[4,32,1,2,32,128]{5,4,3,2,1,0:T(8,128)(2,1)}, u32[]{:S(2)}) copy-start(bf16[4,32,1,2,32,128]{5,4,3,2,1,0:T(8,128)(2,1)} %constant_dynamic-slice_fusion.refs_3_) | copy-start | bytes 6291460
  32.7 10.0 %collective-permute-start.2 = (bf16[16,64,128]{2,1,0:T(8,128)(2,1)S(1)}, bf16[16,64,128]{2,1,0:T(8,128)(2,1)S(1)}, u32[]{:S(2)}, u32[]{:S(2)}) collective-permute-start(bf16[16,64,128]{2,1,0:T(8,128)(2,1)S(1)} %collective-permute-done.refs_0_), channel_id=1, source_target_pairs={{0,32},{32,64},{64,96},{96,0},{1,33},{33,65},{65,97},{97,1},{2,34}... | collective-permute-start | bytes 786440 | tf_op jit(solution)/shard_map/ppermute | solution.py:286
  34.2 10.1 %collective-permute-start.3 = (bf16[16,64,128]{2,1,0:T(8,128)(2,1)S(1)}, bf16[16,64,128]{2,1,0:T(8,128)(2,1)S(1)}, u32[]{:S(2)}, u32[]{:S(2)}) collective-permute-start(bf16[16,64,128]{2,1,0:T(8,128)(2,1)S(1)} %collective-permute-done.1.refs_1_), channel_id=1, source_target_pairs={{0,96},{32,0},{64,32},{96,64},{1,97},{33,1},{65,33},{97,65},{2,98}... | collective-permute-start | bytes 786440 | tf_op jit(solution)/shard_map/ppermute | solution.py:289
  39.3 9.8 %collective-permute-start.4 = (bf16[16,64,128]{2,1,0:T(8,128)(2,1)S(1)}, bf16[16,64,128]{2,1,0:T(8,128)(2,1)S(1)}, u32[]{:S(2)}, u32[]{:S(2)}) collective-permute-start(bf16[16,64,128]{2,1,0:T(8,128)(2,1)S(1)} %get-tuple-element.29), channel_id=1, source_target_pairs={{0,32},{32,64},{64,96},{96,0},{1,33},{33,65},{65,97},{97,1},{2,34}... | collective-permute-start | bytes 786440 | tf_op jit(solution)/shard_map/ppermute | solution.py:286
  39.7 11.4 %collective-permute-start.5 = (bf16[16,64,128]{2,1,0:T(8,128)(2,1)S(1)}, bf16[16,64,128]{2,1,0:T(8,128)(2,1)S(1)}, u32[]{:S(2)}, u32[]{:S(2)}) collective-permute-start(bf16[16,64,128]{2,1,0:T(8,128)(2,1)S(1)} %get-tuple-element.30), channel_id=1, source_target_pairs={{0,96},{32,0},{64,32},{96,64},{1,97},{33,1},{65,33},{97,65},{2,98}... | collective-permute-start | bytes 786440 | tf_op jit(solution)/shard_map/ppermute | solution.py:289
  44.2 10.5 %collective-permute-start.6 = (bf16[16,64,128]{2,1,0:T(8,128)(2,1)S(1)}, bf16[16,64,128]{2,1,0:T(8,128)(2,1)S(1)}, u32[]{:S(2)}, u32[]{:S(2)}) collective-permute-start(bf16[16,64,128]{2,1,0:T(8,128)(2,1)S(1)} %coil_gradient.7), channel_id=1, source_target_pairs={{0,32},{32,64},{64,96},{96,0},{1,33},{33,65},{65,97},{97,1},{2,34}... | collective-permute-start | bytes 786440 | tf_op jit(solution)/shard_map/ppermute | solution.py:286
  45.8 10.0 %collective-permute-start.10 = (bf16[16,64,128]{2,1,0:T(8,128)(2,1)S(1)}, bf16[16,64,128]{2,1,0:T(8,128)(2,1)S(1)}, u32[]{:S(2)}, u32[]{:S(2)}) collective-permute-start(bf16[16,64,128]{2,1,0:T(8,128)(2,1)S(1)} %coil_gradient.8), channel_id=1, source_target_pairs={{0,96},{32,0},{64,32},{96,64},{1,97},{33,1},{65,33},{97,65},{2,98}... | collective-permute-start | bytes 786440 | tf_op jit(solution)/shard_map/ppermute | solution.py:289
  49.1 11.9 %collective-permute-start.8 = (bf16[16,64,128]{2,1,0:T(8,128)(2,1)S(1)}, bf16[16,64,128]{2,1,0:T(8,128)(2,1)S(1)}, u32[]{:S(2)}, u32[]{:S(2)}) collective-permute-start(bf16[16,64,128]{2,1,0:T(8,128)(2,1)S(1)} %get-tuple-element.32), channel_id=1, source_target_pairs={{0,96},{32,0},{64,32},{96,64},{1,97},{33,1},{65,33},{97,65},{2,98}... | collective-permute-start | bytes 786440 | tf_op jit(solution)/shard_map/ppermute | solution.py:289
  49.2 47.7 %copy-start.4 = (f32[2,32,8]{1,2,0:T(8,128)S(1)}, f32[2,32,8]{1,2,0:T(8,128)}, u32[]{:S(2)}) copy-start(f32[2,32,8]{1,2,0:T(8,128)} %param.14) | copy-start | bytes 6148
  49.2 51.9 %copy-start.1 = (f32[1,32,2,32,128]{4,3,2,1,0:T(8,128)S(1)}, f32[1,32,2,32,128]{4,3,2,1,0:T(8,128)}, u32[]{:S(2)}) copy-start(f32[1,32,2,32,128]{4,3,2,1,0:T(8,128)} %param.10) | copy-start | bytes 3145732
  49.2 11.8 %collective-permute-start.9 = (bf16[16,64,128]{2,1,0:T(8,128)(2,1)S(1)}, bf16[16,64,128]{2,1,0:T(8,128)(2,1)S(1)}, u32[]{:S(2)}, u32[]{:S(2)}) collective-permute-start(bf16[16,64,128]{2,1,0:T(8,128)(2,1)S(1)} %get-tuple-element.34), channel_id=1, source_target_pairs={{0,32},{32,64},{64,96},{96,0},{1,33},{33,65},{65,97},{97,1},{2,34}... | collective-permute-start | bytes 786440 | tf_op jit(solution)/shard_map/ppermute | solution.py:286
  54.8 9.5 %collective-permute-start.7 = (bf16[16,64,128]{2,1,0:T(8,128)(2,1)S(1)}, bf16[16,64,128]{2,1,0:T(8,128)(2,1)S(1)}, u32[]{:S(2)}, u32[]{:S(2)}) collective-permute-start(bf16[16,64,128]{2,1,0:T(8,128)(2,1)S(1)} %pair_sum.2), channel_id=1, source_target_pairs={{0,32},{32,64},{64,96},{96,0},{1,33},{33,65},{65,97},{97,1},{2,34}... | collective-permute-start | bytes 786440 | tf_op jit(solution)/shard_map/ppermute | solution.py:286
  55.9 8.3 %collective-permute-start.11 = (bf16[16,64,128]{2,1,0:T(8,128)(2,1)S(1)}, bf16[16,64,128]{2,1,0:T(8,128)(2,1)S(1)}, u32[]{:S(2)}, u32[]{:S(2)}) collective-permute-start(bf16[16,64,128]{2,1,0:T(8,128)(2,1)S(1)} %pair_sum.3), channel_id=1, source_target_pairs={{0,96},{32,0},{64,32},{96,64},{1,97},{33,1},{65,33},{97,65},{2,98}... | collective-permute-start | bytes 786440 | tf_op jit(solution)/shard_map/ppermute | solution.py:289
  92.7 4.6 %collective-permute-start.12 = (f32[8,128]{1,0:T(8,128)S(1)}, f32[8,128]{1,0:T(8,128)S(1)}, u32[]{:S(2)}, u32[]{:S(2)}) collective-permute-start(f32[8,128]{1,0:T(8,128)S(1)} %reduce_sum.9.q0), channel_id=1, source_target_pairs={{0,96},{32,0},{64,32},{96,64},{1,97},{33,1},{65,33},{97,65},{2,98}... | collective-permute-start | bytes 12296 | tf_op jit(solution)/shard_map/ppermute | solution.py:289
  95.9 5.1 %collective-permute-start.13 = (f32[8,128]{1,0:T(8,128)S(1)}, f32[8,128]{1,0:T(8,128)S(1)}, u32[]{:S(2)}, u32[]{:S(2)}) collective-permute-start(f32[8,128]{1,0:T(8,128)S(1)} %reduce_sum.9.q0), channel_id=1, source_target_pairs={{0,64},{32,96},{64,0},{96,32},{1,65},{33,97},{65,1},{97,33},{2,66}... | collective-permute-start | bytes 12296 | tf_op jit(solution)/shard_map/ppermute | solution.py:315
  95.9 5.1 %collective-permute-start.14 = (f32[8,128]{1,0:T(8,128)S(1)}, f32[8,128]{1,0:T(8,128)S(1)}, u32[]{:S(2)}, u32[]{:S(2)}) collective-permute-start(f32[8,128]{1,0:T(8,128)S(1)} %reduce_sum.9.q0), channel_id=1, source_target_pairs={{0,32},{32,64},{64,96},{96,0},{1,33},{33,65},{65,97},{97,1},{2,34}... | collective-permute-start | bytes 12296 | tf_op jit(solution)/shard_map/ppermute | solution.py:286
